TPU v7x, 512 devices: a whole 4x8x8 slice. The times are simulated.
512 devices in a mesh: xy: 128 (over y, z, core), gz: 4 (over x).
Axes of the slice: x: 4, y: 8, z: 8, core: 2. Of those that a mesh axis runs over, the one named last changes fastest.
Arguments:
- right_side: float32 [64, 128, 32, 128], P('gz', 'xy'), may hold values from -4.5 to 4.5
- phase: int32 [64, 128, 32, 128], P('gz', 'xy'), may hold values 0 or 1
- density_scale: float32 [64, 128, 32, 128], P('gz', 'xy'), may hold values from 0.5 to 2
Outputs:
- corrected: float32 [64, 128, 32, 128], P('gz', 'xy')
- coarse_correction: float32 [32, 128, 16, 64], P('gz', 'xy')
All inputs are finite; a program needn't handle non-finite values. No bound on the sum of `phase` on one device may be relied on, other than what follows from the above.
Results may differ from a plain program's by a relative error of at most 0.00002.
Values sent between devices are 32-bit elements; how exact they have to be, the bound alone decides.
A program may use at most 128 MiB of HBM per device.

v0:
```python
import jax
import jax.numpy as jnp
from jax import lax
from jax.sharding import PartitionSpec as P

PY = 8
FINE_SWEEPS = 4
COARSE_SWEEPS = 8


def padded(cells, sides, width):
    for axis, dim in sides:
        count = lax.axis_size(axis)
        ends = count - 1
        head = lax.slice_in_dim(cells, 0, width, axis=dim)
        tail = lax.slice_in_dim(cells, cells.shape[dim] - width, cells.shape[dim], axis=dim)
        cells = jnp.concatenate(
            [
                lax.ppermute(tail, axis, [(i, (i + 1) % count) for i in range(ends)]),
                cells,
                lax.ppermute(head, axis, [((i + 1) % count, i) for i in range(ends)]),
            ],
            axis=dim,
        )
    return cells


def passed_along(shard, axis, by):
    devices = lax.axis_size(axis)
    pairs = [(i, i + by) for i in range(devices) if 0 <= i + by < devices]
    return lax.ppermute(shard, axis, pairs)


def chebyshev_table(low_bound, sweeps):
    middle = 0.5 * (2.0 + low_bound)
    radius = 0.5 * (2.0 - low_bound)
    quotient = middle / radius
    previous = 1.0 / quotient
    coeffs = []
    for number in range(sweeps):
        current = 1.0 / (2.0 * quotient - previous)
        coeffs.append((current * previous, 2.0 * current / radius))
        previous = current
    return (1.0 / middle, coeffs)


def assemble(field, z_wide, x_low, x_high, y_low, y_high):
    return [
        z_wide[:-2],
        z_wide[2:],
        jnp.concatenate([x_low, field[:, :-1]], axis=1),
        jnp.concatenate([field[:, 1:], x_high], axis=1),
        jnp.concatenate([y_low, field[:, :, :-1]], axis=2),
        jnp.concatenate([field[:, :, 1:], y_high], axis=2),
    ]


def mask_rows(y_low, y_high):
    place = lax.axis_index("xy") % PY
    return (jnp.where(place > 0, y_low, 0.0), jnp.where(place < PY - 1, y_high, 0.0))


def fine_beside(field):
    z_wide = padded(field, (("gz", 0),), 1)
    x_low = passed_along(field[:, -1:, :], "xy", PY)
    x_high = passed_along(field[:, :1, :], "xy", -PY)
    y_low = passed_along(field[:, :, -1:], "xy", 1)
    y_high = passed_along(field[:, :, :1], "xy", -1)
    y_low, y_high = mask_rows(y_low, y_high)
    return assemble(field, z_wide, x_low, x_high, y_low, y_high)


def coarse_beside(field):
    z_wide = padded(field, (("gz", 0),), 1)
    x_low = passed_along(field[:, -1:, :], "xy", PY)
    x_high = passed_along(field[:, :1, :], "xy", -PY)
    y_low = passed_along(field[:, :, -1:], "xy", 1)
    y_high = passed_along(field[:, :, :1], "xy", -1)
    y_low, y_high = mask_rows(y_low, y_high)
    return assemble(field, z_wide, x_low, x_high, y_low, y_high)


def face_weights(density, beside_list):
    return jnp.stack([2.0 / (density + beside) for beside in beside_list])


def sum_faces(face_set):
    return face_set[0] + face_set[1] + face_set[2] + face_set[3] + face_set[4] + face_set[5]


def apply_operator(field, beside_list, face_set, diagonal):
    summed = face_set[0] * beside_list[0] + face_set[1] * beside_list[1]
    summed = summed + face_set[2] * beside_list[2] + face_set[3] * beside_list[3]
    summed = summed + face_set[4] * beside_list[4] + face_set[5] * beside_list[5]
    return diagonal * field - summed


def chebyshev(source, face_set, diagonal, low_bound, sweeps, beside_fn):
    inverse_center, coeffs = chebyshev_table(low_bound, sweeps)
    iterate = jnp.zeros_like(source)
    residual = source
    search = residual / diagonal * inverse_center
    for number in range(sweeps):
        iterate = iterate + search
        residual = residual - apply_operator(search, beside_fn(search), face_set, diagonal)
        if number + 1 < sweeps:
            keep_part, push_part = coeffs[number]
            search = keep_part * search + push_part * (residual / diagonal)
    return (iterate, residual)


def restrict_cells(field_in):
    planes, lines, columns = field_in.shape
    blocks = field_in.reshape(planes // 2, 2, lines // 2, 2, columns // 2, 2)
    return jnp.sum(blocks, axis=(1, 3, 5)) * 0.125


def coarsen_faces(face_set):
    planes, lines, columns = face_set.shape[1:]
    half_planes, half_lines, half_columns = (planes // 2, lines // 2, columns // 2)
    low_z = face_set[0][0::2].reshape(half_planes, half_lines, 2, half_columns, 2).sum(axis=(2, 4))
    high_z = face_set[1][1::2].reshape(half_planes, half_lines, 2, half_columns, 2).sum(axis=(2, 4))
    low_x = (
        face_set[2][:, 0::2].reshape(half_planes, 2, half_lines, half_columns, 2).sum(axis=(1, 4))
    )
    high_x = (
        face_set[3][:, 1::2].reshape(half_planes, 2, half_lines, half_columns, 2).sum(axis=(1, 4))
    )
    low_y = (
        face_set[4][:, :, 0::2]
        .reshape(half_planes, 2, half_lines, 2, half_columns)
        .sum(axis=(1, 3))
    )
    high_y = (
        face_set[5][:, :, 1::2]
        .reshape(half_planes, 2, half_lines, 2, half_columns)
        .sum(axis=(1, 3))
    )
    return jnp.stack([low_z, high_z, low_x, high_x, low_y, high_y]) * 0.0625


def prolong_cells(coarse):
    planes, lines, columns = coarse.shape
    spread = jnp.broadcast_to(coarse[:, None, :, None, :, None], (planes, 2, lines, 2, columns, 2))
    return spread.reshape(planes * 2, lines * 2, columns * 2)


def body(right_side, phase, density_scale):
    source = right_side[:, 0]
    density = jnp.where(phase[:, 0] == 1, 1000.0, 1.0).astype(jnp.float32) * density_scale[:, 0]
    face_set = face_weights(density, fine_beside(density))
    diagonal = sum_faces(face_set)
    smoothed, fine_residual = chebyshev(source, face_set, diagonal, 0.5, FINE_SWEEPS, fine_beside)
    coarse_rhs = restrict_cells(fine_residual)
    coarse_faces = coarsen_faces(face_set)
    coarse_diagonal = sum_faces(coarse_faces)
    coarse_field, coarse_residual = chebyshev(
        coarse_rhs, coarse_faces, coarse_diagonal, 0.1, COARSE_SWEEPS, coarse_beside
    )
    corrected = smoothed + prolong_cells(coarse_field)
    return (corrected[:, None], coarse_field[:, None])


def solution(mesh):
    placed = (P("gz", "xy", None, None), P("gz", "xy", None, None), P("gz", "xy", None, None))
    return jax.shard_map(
        body,
        mesh=mesh,
        in_specs=placed,
        out_specs=(P("gz", "xy", None, None), P("gz", "xy", None, None)),
        check_vma=False,
    )
```

profile of v0, /device:TPU:38, one launch (start us, length us, event | category | flops | bytes accessed | tf_op | source)
XLA Modules:
  0.0 440.1 jit_solution(2983989907691836839)
XLA Ops:
  1.7 10.9 %collective-permute-start.2 = (f32[16,1,128]{2,1,0:T(1,128)S(1)}, f32[16,1,128]{2,1,0:T(1,128)S(1)}, u32[]{:S(2)}, u32[]{:S(2)}) collective-permute-start(f32[16,1,128]{2,1,0:T(1,128)S(1)} %get-tuple-element.78), channel_id=1, source_target_pairs={{0,32},{4,36},{8,40},{12,44},{16,48},{20,52},{24,56},{28,60},{32,6... | collective-permute-start | bytes 24584 | tf_op jit(solution)/shard_map/ppermute | solution.py:31
  15.9 4.7 %collective-permute-start.1 = (f32[1,32,128]{2,1,0:T(8,128)S(1)}, f32[1,32,128]{2,1,0:T(8,128)S(1)}, u32[]{:S(2)}, u32[]{:S(2)}) collective-permute-start(f32[1,32,128]{2,1,0:T(8,128)S(1)} %get-tuple-element.77), channel_id=1, source_target_pairs={{1,0},{2,1},{3,2},{5,4},{6,5},{7,6},{9,8},{10,9},{11,10},{13,12},{... | collective-permute-start | bytes 49160 | tf_op jit(solution)/shard_map/ppermute | solution.py:21
  23.7 8.1 %collective-permute-done.4 = f32[16,32,1]{2,1,0:T(8,128)S(1)} collective-permute-done((f32[16,32,1]{2,1,0:T(8,128)S(1)}, f32[16,32,1]{2,1,0:T(8,128)S(1)}, u32[]{:S(2)}, u32[]{:S(2)}) %collective-permute-start.4) | collective-permute-done | bytes 2080 | tf_op jit(solution)/shard_map/ppermute | solution.py:31
  42.1 5.7 %collective-permute-start.8 = (f32[16,1,128]{2,1,0:T(1,128)}, f32[16,1,128]{2,1,0:T(1,128)}, u32[]{:S(2)}, u32[]{:S(2)}) collective-permute-start(f32[16,1,128]{2,1,0:T(1,128)} %get-tuple-element.68), channel_id=1, source_target_pairs={{0,32},{4,36},{8,40},{12,44},{16,48},{20,52},{24,56},{28,60},{32,6... | collective-permute-start | bytes 24584 | tf_op jit(solution)/shard_map/ppermute | solution.py:31
  47.8 6.1 %collective-permute-start.9 = (f32[16,1,128]{2,1,0:T(1,128)}, f32[16,1,128]{2,1,0:T(1,128)}, u32[]{:S(2)}, u32[]{:S(2)}) collective-permute-start(f32[16,1,128]{2,1,0:T(1,128)} %get-tuple-element.69), channel_id=1, source_target_pairs={{32,0},{36,4},{40,8},{44,12},{48,16},{52,20},{56,24},{60,28},{64,3... | collective-permute-start | bytes 24584 | tf_op jit(solution)/shard_map/ppermute | solution.py:31
  55.3 5.1 %collective-permute-start.7 = (f32[1,32,128]{2,1,0:T(8,128)}, f32[1,32,128]{2,1,0:T(8,128)}, u32[]{:S(2)}, u32[]{:S(2)}) collective-permute-start(f32[1,32,128]{2,1,0:T(8,128)} %get-tuple-element.67), channel_id=1, source_target_pairs={{1,0},{2,1},{3,2},{5,4},{6,5},{7,6},{9,8},{10,9},{11,10},{13,12},{... | collective-permute-start | bytes 49160 | tf_op jit(solution)/shard_map/ppermute | solution.py:21
  62.5 6.4 %slice.607 = f32[16,32,64]{2,1,0:T(8,128)S(1)} slice(f32[16,32,128]{2,1,0:T(8,128)S(1)} %get-tuple-element.30), slice={[0:16:1], [0:32:1], [1:128:2]} | slice | bytes 262144 | tf_op jit(solution)/shard_map/slice | solution.py:135
  68.9 6.3 %slice.606 = f32[16,32,64]{2,1,0:T(8,128)S(1)} slice(f32[16,32,128]{2,1,0:T(8,128)S(1)} %get-tuple-element.31), slice={[0:16:1], [0:32:1], [0:128:2]} | slice | bytes 262144 | tf_op jit(solution)/shard_map/slice | solution.py:130
  110.6 7.0 %collective-permute-start.11 = (f32[16,32,1]{2,1,0:T(8,128)}, f32[16,32,1]{2,1,0:T(8,128)S(1)}, u32[]{:S(2)}, u32[]{:S(2)}) collective-permute-start(f32[16,32,1]{2,1,0:T(8,128)} %get-tuple-element.73), channel_id=1, source_target_pairs={{4,0},{8,4},{12,8},{16,12},{20,16},{24,20},{28,24},{32,28},{36,32}... | collective-permute-start | bytes 6152 | tf_op jit(solution)/shard_map/ppermute | solution.py:31
  128.3 9.2 %collective-permute-start.15 = (f32[16,1,128]{2,1,0:T(1,128)S(1)}, f32[16,1,128]{2,1,0:T(1,128)S(1)}, u32[]{:S(2)}, u32[]{:S(2)}) collective-permute-start(f32[16,1,128]{2,1,0:T(1,128)S(1)} %get-tuple-element.59), channel_id=1, source_target_pairs={{32,0},{36,4},{40,8},{44,12},{48,16},{52,20},{56,24},{60,28},{64,3... | collective-permute-start | bytes 24584 | tf_op jit(solution)/shard_map/ppermute | solution.py:31
  138.8 4.5 %collective-permute-start.13 = (f32[1,32,128]{2,1,0:T(8,128)S(1)}, f32[1,32,128]{2,1,0:T(8,128)S(1)}, u32[]{:S(2)}, u32[]{:S(2)}) collective-permute-start(f32[1,32,128]{2,1,0:T(8,128)S(1)} %get-tuple-element.57), channel_id=1, source_target_pairs={{1,0},{2,1},{3,2},{5,4},{6,5},{7,6},{9,8},{10,9},{11,10},{13,12},{... | collective-permute-start | bytes 49160 | tf_op jit(solution)/shard_map/ppermute | solution.py:21
  156.6 9.2 %collective-permute-start.21 = (f32[16,1,128]{2,1,0:T(1,128)S(1)}, f32[16,1,128]{2,1,0:T(1,128)S(1)}, u32[]{:S(2)}, u32[]{:S(2)}) collective-permute-start(f32[16,1,128]{2,1,0:T(1,128)S(1)} %get-tuple-element.49), channel_id=1, source_target_pairs={{32,0},{36,4},{40,8},{44,12},{48,16},{52,20},{56,24},{60,28},{64,3... | collective-permute-start | bytes 24584 | tf_op jit(solution)/shard_map/ppermute | solution.py:31
  167.1 4.5 %collective-permute-start.19 = (f32[1,32,128]{2,1,0:T(8,128)S(1)}, f32[1,32,128]{2,1,0:T(8,128)S(1)}, u32[]{:S(2)}, u32[]{:S(2)}) collective-permute-start(f32[1,32,128]{2,1,0:T(8,128)S(1)} %get-tuple-element.47), channel_id=1, source_target_pairs={{1,0},{2,1},{3,2},{5,4},{6,5},{7,6},{9,8},{10,9},{11,10},{13,12},{... | collective-permute-start | bytes 49160 | tf_op jit(solution)/shard_map/ppermute | solution.py:21
  180.4 7.1 %collective-permute-start.29 = (f32[16,32,1]{2,1,0:T(8,128)S(1)}, f32[16,32,1]{2,1,0:T(8,128)S(1)}, u32[]{:S(2)}, u32[]{:S(2)}) collective-permute-start(f32[16,32,1]{2,1,0:T(8,128)S(1)} %get-tuple-element.38), channel_id=1, source_target_pairs={{4,0},{8,4},{12,8},{16,12},{20,16},{24,20},{28,24},{32,28},{36,32}... | collective-permute-start | bytes 6152 | tf_op jit(solution)/shard_map/ppermute | solution.py:31
  189.5 7.8 %collective-permute-start.26 = (f32[16,1,128]{2,1,0:T(1,128)S(1)}, f32[16,1,128]{2,1,0:T(1,128)S(1)}, u32[]{:S(2)}, u32[]{:S(2)}) collective-permute-start(f32[16,1,128]{2,1,0:T(1,128)S(1)} %get-tuple-element.43), channel_id=1, source_target_pairs={{0,32},{4,36},{8,40},{12,44},{16,48},{20,52},{24,56},{28,60},{32,6... | collective-permute-start | bytes 24584 | tf_op jit(solution)/shard_map/ppermute | solution.py:31
  198.6 4.5 %collective-permute-start.25 = (f32[1,32,128]{2,1,0:T(8,128)S(1)}, f32[1,32,128]{2,1,0:T(8,128)S(1)}, u32[]{:S(2)}, u32[]{:S(2)}) collective-permute-start(f32[1,32,128]{2,1,0:T(8,128)S(1)} %get-tuple-element.45), channel_id=1, source_target_pairs={{1,0},{2,1},{3,2},{5,4},{6,5},{7,6},{9,8},{10,9},{11,10},{13,12},{... | collective-permute-start | bytes 49160 | tf_op jit(solution)/shard_map/ppermute | solution.py:21
  205.3 8.8 %collective-permute-done.28 = f32[16,32,1]{2,1,0:T(8,128)S(1)} collective-permute-done((f32[16,32,1]{2,1,0:T(8,128)S(1)}, f32[16,32,1]{2,1,0:T(8,128)S(1)}, u32[]{:S(2)}, u32[]{:S(2)}) %collective-permute-start.28) | collective-permute-done | bytes 2080 | tf_op jit(solution)/shard_map/ppermute | solution.py:31
  214.7 18.1 %reshape.37 = f32[8,2,16,2,64,2]{5,4,3,2,1,0:T(8,128)} reshape(f32[16,32,128]{2,1,0:T(8,128)S(1)} %fusion.7) | data formatting | bytes 524288 | tf_op jit(solution)/shard_map/reshape | solution.py:114
  232.8 7.0 %reduce_sum.63 = f32[8,16,64]{2,1,0:T(8,128)S(1)} reduce(f32[8,2,16,2,64,2]{5,4,3,2,1,0:T(8,128)} %reshape.37, f32[]{:T(128)} %constant.78.clone.1), dimensions={1,3,5}, to_apply=%region_0.1 | reduce | flops 57344 | bytes 294916 | tf_op jit(solution)/shard_map/reduce_sum | solution.py:115
  243.9 9.9 %collective-permute-start.33 = (f32[8,1,64]{2,1,0:T(1,128)S(1)}, f32[8,1,64]{2,1,0:T(1,128)S(1)}, u32[]{:S(2)}, u32[]{:S(2)}) collective-permute-start(f32[8,1,64]{2,1,0:T(1,128)S(1)} %get-tuple-element.149), channel_id=1, source_target_pairs={{32,0},{36,4},{40,8},{44,12},{48,16},{52,20},{56,24},{60,28},{64,3... | collective-permute-start | bytes 6152 | tf_op jit(solution)/shard_map/ppermute | solution.py:31
  255.1 4.5 %collective-permute-start.31 = (f32[1,16,64]{2,1,0:T(8,128)S(1)}, f32[1,16,64]{2,1,0:T(8,128)S(1)}, u32[]{:S(2)}, u32[]{:S(2)}) collective-permute-start(f32[1,16,64]{2,1,0:T(8,128)S(1)} %get-tuple-element.147), channel_id=1, source_target_pairs={{1,0},{2,1},{3,2},{5,4},{6,5},{7,6},{9,8},{10,9},{11,10},{13,12},{... | collective-permute-start | bytes 12296 | tf_op jit(solution)/shard_map/ppermute | solution.py:21
  269.9 9.7 %collective-permute-start.39 = (f32[8,1,64]{2,1,0:T(1,128)S(1)}, f32[8,1,64]{2,1,0:T(1,128)S(1)}, u32[]{:S(2)}, u32[]{:S(2)}) collective-permute-start(f32[8,1,64]{2,1,0:T(1,128)S(1)} %get-tuple-element.139), channel_id=1, source_target_pairs={{32,0},{36,4},{40,8},{44,12},{48,16},{52,20},{56,24},{60,28},{64,3... | collective-permute-start | bytes 6152 | tf_op jit(solution)/shard_map/ppermute | solution.py:31
  280.8 4.5 %collective-permute-start.37 = (f32[1,16,64]{2,1,0:T(8,128)S(1)}, f32[1,16,64]{2,1,0:T(8,128)S(1)}, u32[]{:S(2)}, u32[]{:S(2)}) collective-permute-start(f32[1,16,64]{2,1,0:T(8,128)S(1)} %get-tuple-element.137), channel_id=1, source_target_pairs={{1,0},{2,1},{3,2},{5,4},{6,5},{7,6},{9,8},{10,9},{11,10},{13,12},{... | collective-permute-start | bytes 12296 | tf_op jit(solution)/shard_map/ppermute | solution.py:21
  295.6 9.7 %collective-permute-start.45 = (f32[8,1,64]{2,1,0:T(1,128)S(1)}, f32[8,1,64]{2,1,0:T(1,128)S(1)}, u32[]{:S(2)}, u32[]{:S(2)}) collective-permute-start(f32[8,1,64]{2,1,0:T(1,128)S(1)} %get-tuple-element.129), channel_id=1, source_target_pairs={{32,0},{36,4},{40,8},{44,12},{48,16},{52,20},{56,24},{60,28},{64,3... | collective-permute-start | bytes 6152 | tf_op jit(solution)/shard_map/ppermute | solution.py:31
  306.6 4.5 %collective-permute-start.43 = (f32[1,16,64]{2,1,0:T(8,128)S(1)}, f32[1,16,64]{2,1,0:T(8,128)S(1)}, u32[]{:S(2)}, u32[]{:S(2)}) collective-permute-start(f32[1,16,64]{2,1,0:T(8,128)S(1)} %get-tuple-element.127), channel_id=1, source_target_pairs={{1,0},{2,1},{3,2},{5,4},{6,5},{7,6},{9,8},{10,9},{11,10},{13,12},{... | collective-permute-start | bytes 12296 | tf_op jit(solution)/shard_map/ppermute | solution.py:21
  321.4 9.7 %collective-permute-start.51 = (f32[8,1,64]{2,1,0:T(1,128)S(1)}, f32[8,1,64]{2,1,0:T(1,128)S(1)}, u32[]{:S(2)}, u32[]{:S(2)}) collective-permute-start(f32[8,1,64]{2,1,0:T(1,128)S(1)} %get-tuple-element.119), channel_id=1, source_target_pairs={{32,0},{36,4},{40,8},{44,12},{48,16},{52,20},{56,24},{60,28},{64,3... | collective-permute-start | bytes 6152 | tf_op jit(solution)/shard_map/ppermute | solution.py:31
  332.4 4.5 %collective-permute-start.49 = (f32[1,16,64]{2,1,0:T(8,128)S(1)}, f32[1,16,64]{2,1,0:T(8,128)S(1)}, u32[]{:S(2)}, u32[]{:S(2)}) collective-permute-start(f32[1,16,64]{2,1,0:T(8,128)S(1)} %get-tuple-element.117), channel_id=1, source_target_pairs={{1,0},{2,1},{3,2},{5,4},{6,5},{7,6},{9,8},{10,9},{11,10},{13,12},{... | collective-permute-start | bytes 12296 | tf_op jit(solution)/shard_map/ppermute | solution.py:21
  347.2 9.7 %collective-permute-start.57 = (f32[8,1,64]{2,1,0:T(1,128)S(1)}, f32[8,1,64]{2,1,0:T(1,128)S(1)}, u32[]{:S(2)}, u32[]{:S(2)}) collective-permute-start(f32[8,1,64]{2,1,0:T(1,128)S(1)} %get-tuple-element.109), channel_id=1, source_target_pairs={{32,0},{36,4},{40,8},{44,12},{48,16},{52,20},{56,24},{60,28},{64,3... | collective-permute-start | bytes 6152 | tf_op jit(solution)/shard_map/ppermute | solution.py:31
  372.9 9.7 %collective-permute-start.63 = (f32[8,1,64]{2,1,0:T(1,128)S(1)}, f32[8,1,64]{2,1,0:T(1,128)S(1)}, u32[]{:S(2)}, u32[]{:S(2)}) collective-permute-start(f32[8,1,64]{2,1,0:T(1,128)S(1)} %get-tuple-element.99), channel_id=1, source_target_pairs={{32,0},{36,4},{40,8},{44,12},{48,16},{52,20},{56,24},{60,28},{64,3... | collective-permute-start | bytes 6152 | tf_op jit(solution)/shard_map/ppermute | solution.py:31
  398.6 9.7 %collective-permute-start.69 = (f32[8,1,64]{2,1,0:T(1,128)S(1)}, f32[8,1,64]{2,1,0:T(1,128)S(1)}, u32[]{:S(2)}, u32[]{:S(2)}) collective-permute-start(f32[8,1,64]{2,1,0:T(1,128)S(1)} %get-tuple-element.89), channel_id=1, source_target_pairs={{32,0},{36,4},{40,8},{44,12},{48,16},{52,20},{56,24},{60,28},{64,3... | collective-permute-start | bytes 6152 | tf_op jit(solution)/shard_map/ppermute | solution.py:31
  420.0 6.6 %broadcast_in_dim.54 = f32[8,2,16,2,64,2]{5,4,3,2,1,0:T(8,128)} broadcast(f32[8,16,64]{2,1,0:T(8,128)S(1)} %add_add_fusion.1), dimensions={0,2,4} | broadcast | bytes 294912 | tf_op jit(solution)/shard_map/broadcast_in_dim | solution.py:144
  426.6 12.6 %reshape.44 = f32[16,32,128]{2,1,0:T(8,128)S(1)} reshape(f32[8,2,16,2,64,2]{5,4,3,2,1,0:T(8,128)} %broadcast_in_dim.54) | data formatting | bytes 524288 | tf_op jit(solution)/shard_map/reshape | solution.py:145
  (246 shorter events, 191.3 us)
Async XLA Ops:
  1.7 35.8 %collective-permute-start.2 = (f32[16,1,128]{2,1,0:T(1,128)S(1)}, f32[16,1,128]{2,1,0:T(1,128)S(1)}, u32[]{:S(2)}, u32[]{:S(2)}) collective-permute-start(f32[16,1,128]{2,1,0:T(1,128)S(1)} %get-tuple-element.78), channel_id=1, source_target_pairs={{0,32},{4,36},{8,40},{12,44},{16,48},{20,52},{24,56},{28,60},{32,6... | collective-permute-start | bytes 24584 | tf_op jit(solution)/shard_map/ppermute | solution.py:31
  12.6 24.9 %collective-permute-start.3 = (f32[16,1,128]{2,1,0:T(1,128)S(1)}, f32[16,1,128]{2,1,0:T(1,128)S(1)}, u32[]{:S(2)}, u32[]{:S(2)}) collective-permute-start(f32[16,1,128]{2,1,0:T(1,128)S(1)} %get-tuple-element.79), channel_id=1, source_target_pairs={{32,0},{36,4},{40,8},{44,12},{48,16},{52,20},{56,24},{60,28},{64,3... | collective-permute-start | bytes 24584 | tf_op jit(solution)/shard_map/ppermute | solution.py:31
  14.6 23.0 %collective-permute-start = (f32[1,32,128]{2,1,0:T(8,128)S(1)}, f32[1,32,128]{2,1,0:T(8,128)S(1)}, u32[]{:S(2)}, u32[]{:S(2)}) collective-permute-start(f32[1,32,128]{2,1,0:T(8,128)S(1)} %get-tuple-element.76), channel_id=1, source_target_pairs={{0,1},{1,2},{2,3},{4,5},{5,6},{6,7},{8,9},{9,10},{10,11},{12,13},{... | collective-permute-start | bytes 49160 | tf_op jit(solution)/shard_map/ppermute | solution.py:19
  15.9 21.7 %collective-permute-start.1 = (f32[1,32,128]{2,1,0:T(8,128)S(1)}, f32[1,32,128]{2,1,0:T(8,128)S(1)}, u32[]{:S(2)}, u32[]{:S(2)}) collective-permute-start(f32[1,32,128]{2,1,0:T(8,128)S(1)} %get-tuple-element.77), channel_id=1, source_target_pairs={{1,0},{2,1},{3,2},{5,4},{6,5},{7,6},{9,8},{10,9},{11,10},{13,12},{... | collective-permute-start | bytes 49160 | tf_op jit(solution)/shard_map/ppermute | solution.py:21
  42.1 79.7 %collective-permute-start.8 = (f32[16,1,128]{2,1,0:T(1,128)}, f32[16,1,128]{2,1,0:T(1,128)}, u32[]{:S(2)}, u32[]{:S(2)}) collective-permute-start(f32[16,1,128]{2,1,0:T(1,128)} %get-tuple-element.68), channel_id=1, source_target_pairs={{0,32},{4,36},{8,40},{12,44},{16,48},{20,52},{24,56},{28,60},{32,6... | collective-permute-start | bytes 24584 | tf_op jit(solution)/shard_map/ppermute | solution.py:31
  47.8 74.0 %collective-permute-start.9 = (f32[16,1,128]{2,1,0:T(1,128)}, f32[16,1,128]{2,1,0:T(1,128)}, u32[]{:S(2)}, u32[]{:S(2)}) collective-permute-start(f32[16,1,128]{2,1,0:T(1,128)} %get-tuple-element.69), channel_id=1, source_target_pairs={{32,0},{36,4},{40,8},{44,12},{48,16},{52,20},{56,24},{60,28},{64,3... | collective-permute-start | bytes 24584 | tf_op jit(solution)/shard_map/ppermute | solution.py:31
  54.0 67.8 %collective-permute-start.6 = (f32[1,32,128]{2,1,0:T(8,128)}, f32[1,32,128]{2,1,0:T(8,128)S(1)}, u32[]{:S(2)}, u32[]{:S(2)}) collective-permute-start(f32[1,32,128]{2,1,0:T(8,128)} %get-tuple-element.66), channel_id=1, source_target_pairs={{0,1},{1,2},{2,3},{4,5},{5,6},{6,7},{8,9},{9,10},{10,11},{12,13},{... | collective-permute-start | bytes 49160 | tf_op jit(solution)/shard_map/ppermute | solution.py:19
  55.3 66.5 %collective-permute-start.7 = (f32[1,32,128]{2,1,0:T(8,128)}, f32[1,32,128]{2,1,0:T(8,128)}, u32[]{:S(2)}, u32[]{:S(2)}) collective-permute-start(f32[1,32,128]{2,1,0:T(8,128)} %get-tuple-element.67), channel_id=1, source_target_pairs={{1,0},{2,1},{3,2},{5,4},{6,5},{7,6},{9,8},{10,9},{11,10},{13,12},{... | collective-permute-start | bytes 49160 | tf_op jit(solution)/shard_map/ppermute | solution.py:21
  76.9 33.7 %collective-permute-start.10 = (f32[16,32,1]{2,1,0:T(8,128)}, f32[16,32,1]{2,1,0:T(8,128)}, u32[]{:S(2)}, u32[]{:S(2)}) collective-permute-start(f32[16,32,1]{2,1,0:T(8,128)} %get-tuple-element.72), channel_id=1, source_target_pairs={{0,4},{4,8},{8,12},{12,16},{16,20},{20,24},{24,28},{28,32},{32,36}... | collective-permute-start | bytes 6152 | tf_op jit(solution)/shard_map/ppermute | solution.py:31
  123.7 19.7 %collective-permute-start.16 = (f32[16,32,1]{2,1,0:T(8,128)S(1)}, f32[16,32,1]{2,1,0:T(8,128)S(1)}, u32[]{:S(2)}, u32[]{:S(2)}) collective-permute-start(f32[16,32,1]{2,1,0:T(8,128)S(1)} %get-tuple-element.62), channel_id=1, source_target_pairs={{0,4},{4,8},{8,12},{12,16},{16,20},{20,24},{24,28},{28,32},{32,36}... | collective-permute-start | bytes 6152 | tf_op jit(solution)/shard_map/ppermute | solution.py:31
  125.7 25.4 %collective-permute-start.14 = (f32[16,1,128]{2,1,0:T(1,128)S(1)}, f32[16,1,128]{2,1,0:T(1,128)S(1)}, u32[]{:S(2)}, u32[]{:S(2)}) collective-permute-start(f32[16,1,128]{2,1,0:T(1,128)S(1)} %get-tuple-element.58), channel_id=1, source_target_pairs={{0,32},{4,36},{8,40},{12,44},{16,48},{20,52},{24,56},{28,60},{32,6... | collective-permute-start | bytes 24584 | tf_op jit(solution)/shard_map/ppermute | solution.py:31
  128.3 22.8 %collective-permute-start.15 = (f32[16,1,128]{2,1,0:T(1,128)S(1)}, f32[16,1,128]{2,1,0:T(1,128)S(1)}, u32[]{:S(2)}, u32[]{:S(2)}) collective-permute-start(f32[16,1,128]{2,1,0:T(1,128)S(1)} %get-tuple-element.59), channel_id=1, source_target_pairs={{32,0},{36,4},{40,8},{44,12},{48,16},{52,20},{56,24},{60,28},{64,3... | collective-permute-start | bytes 24584 | tf_op jit(solution)/shard_map/ppermute | solution.py:31
  152.0 19.7 %collective-permute-start.22 = (f32[16,32,1]{2,1,0:T(8,128)S(1)}, f32[16,32,1]{2,1,0:T(8,128)S(1)}, u32[]{:S(2)}, u32[]{:S(2)}) collective-permute-start(f32[16,32,1]{2,1,0:T(8,128)S(1)} %get-tuple-element.52), channel_id=1, source_target_pairs={{0,4},{4,8},{8,12},{12,16},{16,20},{20,24},{24,28},{28,32},{32,36}... | collective-permute-start | bytes 6152 | tf_op jit(solution)/shard_map/ppermute | solution.py:31
  153.9 25.5 %collective-permute-start.20 = (f32[16,1,128]{2,1,0:T(1,128)S(1)}, f32[16,1,128]{2,1,0:T(1,128)S(1)}, u32[]{:S(2)}, u32[]{:S(2)}) collective-permute-start(f32[16,1,128]{2,1,0:T(1,128)S(1)} %get-tuple-element.48), channel_id=1, source_target_pairs={{0,32},{4,36},{8,40},{12,44},{16,48},{20,52},{24,56},{28,60},{32,6... | collective-permute-start | bytes 24584 | tf_op jit(solution)/shard_map/ppermute | solution.py:31
  156.6 22.9 %collective-permute-start.21 = (f32[16,1,128]{2,1,0:T(1,128)S(1)}, f32[16,1,128]{2,1,0:T(1,128)S(1)}, u32[]{:S(2)}, u32[]{:S(2)}) collective-permute-start(f32[16,1,128]{2,1,0:T(1,128)S(1)} %get-tuple-element.49), channel_id=1, source_target_pairs={{32,0},{36,4},{40,8},{44,12},{48,16},{52,20},{56,24},{60,28},{64,3... | collective-permute-start | bytes 24584 | tf_op jit(solution)/shard_map/ppermute | solution.py:31
  180.4 22.8 %collective-permute-start.29 = (f32[16,32,1]{2,1,0:T(8,128)S(1)}, f32[16,32,1]{2,1,0:T(8,128)S(1)}, u32[]{:S(2)}, u32[]{:S(2)}) collective-permute-start(f32[16,32,1]{2,1,0:T(8,128)S(1)} %get-tuple-element.38), channel_id=1, source_target_pairs={{4,0},{8,4},{12,8},{16,12},{20,16},{24,20},{28,24},{32,28},{36,32}... | collective-permute-start | bytes 6152 | tf_op jit(solution)/shard_map/ppermute | solution.py:31
  187.5 26.7 %collective-permute-start.27 = (f32[16,1,128]{2,1,0:T(1,128)S(1)}, f32[16,1,128]{2,1,0:T(1,128)S(1)}, u32[]{:S(2)}, u32[]{:S(2)}) collective-permute-start(f32[16,1,128]{2,1,0:T(1,128)S(1)} %get-tuple-element.42), channel_id=1, source_target_pairs={{32,0},{36,4},{40,8},{44,12},{48,16},{52,20},{56,24},{60,28},{64,3... | collective-permute-start | bytes 24584 | tf_op jit(solution)/shard_map/ppermute | solution.py:31
  189.5 24.8 %collective-permute-start.26 = (f32[16,1,128]{2,1,0:T(1,128)S(1)}, f32[16,1,128]{2,1,0:T(1,128)S(1)}, u32[]{:S(2)}, u32[]{:S(2)}) collective-permute-start(f32[16,1,128]{2,1,0:T(1,128)S(1)} %get-tuple-element.43), channel_id=1, source_target_pairs={{0,32},{4,36},{8,40},{12,44},{16,48},{20,52},{24,56},{28,60},{32,6... | collective-permute-start | bytes 24584 | tf_op jit(solution)/shard_map/ppermute | solution.py:31
  242.0 23.4 %collective-permute-start.32 = (f32[8,1,64]{2,1,0:T(1,128)S(1)}, f32[8,1,64]{2,1,0:T(1,128)S(1)}, u32[]{:S(2)}, u32[]{:S(2)}) collective-permute-start(f32[8,1,64]{2,1,0:T(1,128)S(1)} %get-tuple-element.148), channel_id=1, source_target_pairs={{0,32},{4,36},{8,40},{12,44},{16,48},{20,52},{24,56},{28,60},{32,6... | collective-permute-start | bytes 6152 | tf_op jit(solution)/shard_map/ppermute | solution.py:31
  243.9 21.5 %collective-permute-start.33 = (f32[8,1,64]{2,1,0:T(1,128)S(1)}, f32[8,1,64]{2,1,0:T(1,128)S(1)}, u32[]{:S(2)}, u32[]{:S(2)}) collective-permute-start(f32[8,1,64]{2,1,0:T(1,128)S(1)} %get-tuple-element.149), channel_id=1, source_target_pairs={{32,0},{36,4},{40,8},{44,12},{48,16},{52,20},{56,24},{60,28},{64,3... | collective-permute-start | bytes 6152 | tf_op jit(solution)/shard_map/ppermute | solution.py:31
  267.7 23.4 %collective-permute-start.38 = (f32[8,1,64]{2,1,0:T(1,128)S(1)}, f32[8,1,64]{2,1,0:T(1,128)S(1)}, u32[]{:S(2)}, u32[]{:S(2)}) collective-permute-start(f32[8,1,64]{2,1,0:T(1,128)S(1)} %get-tuple-element.138), channel_id=1, source_target_pairs={{0,32},{4,36},{8,40},{12,44},{16,48},{20,52},{24,56},{28,60},{32,6... | collective-permute-start | bytes 6152 | tf_op jit(solution)/shard_map/ppermute | solution.py:31
  269.9 21.2 %collective-permute-start.39 = (f32[8,1,64]{2,1,0:T(1,128)S(1)}, f32[8,1,64]{2,1,0:T(1,128)S(1)}, u32[]{:S(2)}, u32[]{:S(2)}) collective-permute-start(f32[8,1,64]{2,1,0:T(1,128)S(1)} %get-tuple-element.139), channel_id=1, source_target_pairs={{32,0},{36,4},{40,8},{44,12},{48,16},{52,20},{56,24},{60,28},{64,3... | collective-permute-start | bytes 6152 | tf_op jit(solution)/shard_map/ppermute | solution.py:31
  293.4 23.5 %collective-permute-start.44 = (f32[8,1,64]{2,1,0:T(1,128)S(1)}, f32[8,1,64]{2,1,0:T(1,128)S(1)}, u32[]{:S(2)}, u32[]{:S(2)}) collective-permute-start(f32[8,1,64]{2,1,0:T(1,128)S(1)} %get-tuple-element.128), channel_id=1, source_target_pairs={{0,32},{4,36},{8,40},{12,44},{16,48},{20,52},{24,56},{28,60},{32,6... | collective-permute-start | bytes 6152 | tf_op jit(solution)/shard_map/ppermute | solution.py:31
  295.6 21.3 %collective-permute-start.45 = (f32[8,1,64]{2,1,0:T(1,128)S(1)}, f32[8,1,64]{2,1,0:T(1,128)S(1)}, u32[]{:S(2)}, u32[]{:S(2)}) collective-permute-start(f32[8,1,64]{2,1,0:T(1,128)S(1)} %get-tuple-element.129), channel_id=1, source_target_pairs={{32,0},{36,4},{40,8},{44,12},{48,16},{52,20},{56,24},{60,28},{64,3... | collective-permute-start | bytes 6152 | tf_op jit(solution)/shard_map/ppermute | solution.py:31
  319.2 23.4 %collective-permute-start.50 = (f32[8,1,64]{2,1,0:T(1,128)S(1)}, f32[8,1,64]{2,1,0:T(1,128)S(1)}, u32[]{:S(2)}, u32[]{:S(2)}) collective-permute-start(f32[8,1,64]{2,1,0:T(1,128)S(1)} %get-tuple-element.118), channel_id=1, source_target_pairs={{0,32},{4,36},{8,40},{12,44},{16,48},{20,52},{24,56},{28,60},{32,6... | collective-permute-start | bytes 6152 | tf_op jit(solution)/shard_map/ppermute | solution.py:31
  321.4 21.2 %collective-permute-start.51 = (f32[8,1,64]{2,1,0:T(1,128)S(1)}, f32[8,1,64]{2,1,0:T(1,128)S(1)}, u32[]{:S(2)}, u32[]{:S(2)}) collective-permute-start(f32[8,1,64]{2,1,0:T(1,128)S(1)} %get-tuple-element.119), channel_id=1, source_target_pairs={{32,0},{36,4},{40,8},{44,12},{48,16},{52,20},{56,24},{60,28},{64,3... | collective-permute-start | bytes 6152 | tf_op jit(solution)/shard_map/ppermute | solution.py:31
  344.9 23.4 %collective-permute-start.56 = (f32[8,1,64]{2,1,0:T(1,128)S(1)}, f32[8,1,64]{2,1,0:T(1,128)S(1)}, u32[]{:S(2)}, u32[]{:S(2)}) collective-permute-start(f32[8,1,64]{2,1,0:T(1,128)S(1)} %get-tuple-element.108), channel_id=1, source_target_pairs={{0,32},{4,36},{8,40},{12,44},{16,48},{20,52},{24,56},{28,60},{32,6... | collective-permute-start | bytes 6152 | tf_op jit(solution)/shard_map/ppermute | solution.py:31
  347.2 21.2 %collective-permute-start.57 = (f32[8,1,64]{2,1,0:T(1,128)S(1)}, f32[8,1,64]{2,1,0:T(1,128)S(1)}, u32[]{:S(2)}, u32[]{:S(2)}) collective-permute-start(f32[8,1,64]{2,1,0:T(1,128)S(1)} %get-tuple-element.109), channel_id=1, source_target_pairs={{32,0},{36,4},{40,8},{44,12},{48,16},{52,20},{56,24},{60,28},{64,3... | collective-permute-start | bytes 6152 | tf_op jit(solution)/shard_map/ppermute | solution.py:31
  370.7 23.4 %collective-permute-start.62 = (f32[8,1,64]{2,1,0:T(1,128)S(1)}, f32[8,1,64]{2,1,0:T(1,128)S(1)}, u32[]{:S(2)}, u32[]{:S(2)}) collective-permute-start(f32[8,1,64]{2,1,0:T(1,128)S(1)} %get-tuple-element.98), channel_id=1, source_target_pairs={{0,32},{4,36},{8,40},{12,44},{16,48},{20,52},{24,56},{28,60},{32,6... | collective-permute-start | bytes 6152 | tf_op jit(solution)/shard_map/ppermute | solution.py:31
  372.9 21.2 %collective-permute-start.63 = (f32[8,1,64]{2,1,0:T(1,128)S(1)}, f32[8,1,64]{2,1,0:T(1,128)S(1)}, u32[]{:S(2)}, u32[]{:S(2)}) collective-permute-start(f32[8,1,64]{2,1,0:T(1,128)S(1)} %get-tuple-element.99), channel_id=1, source_target_pairs={{32,0},{36,4},{40,8},{44,12},{48,16},{52,20},{56,24},{60,28},{64,3... | collective-permute-start | bytes 6152 | tf_op jit(solution)/shard_map/ppermute | solution.py:31
  396.4 23.4 %collective-permute-start.68 = (f32[8,1,64]{2,1,0:T(1,128)S(1)}, f32[8,1,64]{2,1,0:T(1,128)S(1)}, u32[]{:S(2)}, u32[]{:S(2)}) collective-permute-start(f32[8,1,64]{2,1,0:T(1,128)S(1)} %get-tuple-element.88), channel_id=1, source_target_pairs={{0,32},{4,36},{8,40},{12,44},{16,48},{20,52},{24,56},{28,60},{32,6... | collective-permute-start | bytes 6152 | tf_op jit(solution)/shard_map/ppermute | solution.py:31
  398.6 21.2 %collective-permute-start.69 = (f32[8,1,64]{2,1,0:T(1,128)S(1)}, f32[8,1,64]{2,1,0:T(1,128)S(1)}, u32[]{:S(2)}, u32[]{:S(2)}) collective-permute-start(f32[8,1,64]{2,1,0:T(1,128)S(1)} %get-tuple-element.89), channel_id=1, source_target_pairs={{32,0},{36,4},{40,8},{44,12},{48,16},{52,20},{56,24},{60,28},{64,3... | collective-permute-start | bytes 6152 | tf_op jit(solution)/shard_map/ppermute | solution.py:31
  (42 other events, 594.7 us)
where the time goes:
time: 443 us; the launch traced here: 440 us
  starting transfers between devices  286 us (65%)
  local copies, waits for them, and re-layouts  78.2 us (18%)
  waiting for transfers between devices  45.8 us (10%)
  other arithmetic  28.2 us (6%)
    ppermute x48, starting transfers between devices, passed_along(): return lax.ppermute(shard, axis, pairs)  215 us
    ppermute x12, starting transfers between devices, padded(): lax.ppermute(head, axis, [((i + 1) % count, i) for i in range(ends)])  55.3 us
    ppermute x48, waiting for transfers between devices, passed_along(): return lax.ppermute(shard, axis, pairs)  45.7 us
    reshape x1, local copies, waits for them, and re-layouts, restrict_cells(): blocks = field_in.reshape(planes // 2, 2, lines // 2, 2, columns // 2, 2)  18.1 us
    ppermute x12, starting transfers between devices, padded(): lax.ppermute(tail, axis, [(i, (i + 1) % count) for i in range(ends)])  15.5 us
    reshape x1, local copies, waits for them, and re-layouts, prolong_cells(): return spread.reshape(planes * 2, lines * 2, columns * 2)  12.6 us
  transfers between devices with their start and end apart: 72, of which 13 were waited for; matrix products, arithmetic and copies ran while one was open for 11% of the time, Pallas kernels for 0%

commit v1 on v0

v1 whole, which is shorter than its diff:
```python
import jax
import jax.numpy as jnp
from jax import lax
from jax.experimental import pallas as pl
from jax.experimental.pallas import tpu as pltpu
from jax.sharding import PartitionSpec as P

PY = 8
FINE_SWEEPS = 4
COARSE_SWEEPS = 8

NZ, BX, BY = 16, 32, 128
HZ = 5
EZ, EX = NZ + 2 * HZ, BX + 16
X0 = 8
CZ, CX, CY = 8, 16, 64
KZ, KX = CZ + 16, CX + 16


def chebyshev_table(low_bound, sweeps):
    middle = 0.5 * (2.0 + low_bound)
    radius = 0.5 * (2.0 - low_bound)
    quotient = middle / radius
    previous = 1.0 / quotient
    coeffs = []
    for number in range(sweeps):
        current = 1.0 / (2.0 * quotient - previous)
        coeffs.append((current * previous, 2.0 * current / radius))
        previous = current
    return (1.0 / middle, coeffs)


def lanes_of(rows):
    return lax.broadcasted_iota(jnp.int32, (rows, 128), 1)


def guarded(total):
    return jnp.where(total > 0.0, 2.0 / total, 0.0)


def kernel(
    right_ref, phase_ref, scale_ref, out_ref, coarse_ref,
    e0, e1, s0, s1, fz0, fz1, fx0, fx1, fy0, fy1, ig0, ig1, xs,
    xsend, xrecv, pack, unpack, stage,
    cs, cr, csx, ys, yr, cx,
    send_sem, recv_sem,
):
    b = lax.axis_index("xy")
    g = lax.axis_index("gz")
    row, col = b // PY, b % PY
    n_rows = lax.axis_size("xy") // PY
    n_gz = lax.axis_size("gz")
    there = ((g > 0, g < n_gz - 1), (row > 0, row < n_rows - 1), (col > 0, col < PY - 1))

    def neighbour(axis, side):
        by = 1 if side else -1
        if axis == 0:
            return {"xy": b, "gz": g + by}
        return {"xy": b + by * (PY if axis == 1 else 1), "gz": g}

    def exchange(number, axis, sources, targets):
        copies = []
        for side in (0, 1):
            index = 2 * number + side
            copies.append(
                pltpu.make_async_remote_copy(
                    src_ref=sources[side], dst_ref=targets[side],
                    send_sem=send_sem.at[index], recv_sem=recv_sem.at[index],
                    device_id=neighbour(axis, side), device_id_type=pl.DeviceIdType.MESH,
                )
            )

        def start():
            for side in (0, 1):
                pl.when(there[axis][side])(copies[side].start)

        def wait():
            for side in (0, 1):
                pl.when(there[axis][1 - side])(copies[side].wait_recv)
            for side in (0, 1):
                pl.when(there[axis][side])(copies[side].wait_send)

        return start, wait

    @pl.loop(0, EZ)
    def _(p):
        for f in (0, 1):
            e0[f, p] = jnp.zeros((EX, 128), jnp.float32)

    barrier = pltpu.get_barrier_semaphore()
    count = jnp.int32(0)
    for axis in (0, 1, 2):
        for side in (0, 1):
            count = count + there[axis][side].astype(jnp.int32)

            @pl.when(there[axis][side])
            def _():
                pl.semaphore_signal(
                    barrier, inc=1, device_id=neighbour(axis, side),
                    device_id_type=pl.DeviceIdType.MESH,
                )

    @pl.loop(0, NZ)
    def _(z):
        heavy = jnp.where(phase_ref[z, 0] == 1, 1000.0, 1.0).astype(jnp.float32)
        e0[0, HZ + z, X0:X0 + BX] = heavy * scale_ref[z, 0]
        e0[1, HZ + z, X0:X0 + BX] = right_ref[z, 0]

    @pl.loop(0, KZ)
    def _(p):
        for f in range(4):
            cs[f, p] = jnp.zeros((KX, 128), jnp.float32)
        cr[p] = jnp.zeros((KX, 128), jnp.float32)

    for j in range(9):
        f, at = (0, j) if j < 5 else (1, j - 5)
        width = 5 - f
        xsend[0, j] = e0[f, HZ:HZ + NZ, X0 + at, :]
        xsend[1, j] = e0[f, HZ:HZ + NZ, X0 + BX - width + at, :]

    pl.semaphore_wait(barrier, count)

    start, wait = exchange(0, 1, (xsend.at[0], xsend.at[1]), (xrecv.at[0], xrecv.at[1]))
    start()
    wait()
    for side in (0, 1):
        @pl.when(there[1][1 - side])
        def _():
            for j in range(9):
                f, at = (0, j) if j < 5 else (1, j - 5)
                width = 5 - f
                to = X0 + BX + at if side == 0 else X0 - width + at
                e0[f, HZ:HZ + NZ, to, :] = xrecv[side, j]

    start, wait = exchange(
        1, 0,
        (e0.at[:, pl.ds(HZ, HZ)], e0.at[:, pl.ds(NZ, HZ)]),
        (e0.at[:, pl.ds(HZ + NZ, HZ)], e0.at[:, pl.ds(0, HZ)]),
    )
    start()
    wait()

    lane = lanes_of(EX)

    @pl.loop(0, EZ)
    def _(p):
        a, at = p // 8, (p % 8) * 16
        d, r = e0[0, p], e0[1, p]
        in_d = (lane >= at) & (lane < at + 8)
        in_r = (lane >= at + 8) & (lane < at + 16)
        for side, extra in ((0, 0), (1, 8)):
            rolled_d = pltpu.roll(d, (at + extra) % 128, 1)
            rolled_r = pltpu.roll(r, (at + extra + 8) % 128, 1)
            pack[side, a] = jnp.where(in_d, rolled_d, jnp.where(in_r, rolled_r, pack[side, a]))

    start, wait = exchange(2, 2, (pack.at[0], pack.at[1]), (unpack.at[0], unpack.at[1]))
    start()
    wait()

    @pl.loop(0, EZ)
    def _(p):
        a, at = p // 8, (p % 8) * 16
        right, left = unpack[0, a], unpack[1, a]
        use_right = (lane < 8) & there[2][1]
        use_left = (lane >= 120) & there[2][0]
        for f in (0, 1):
            low = pltpu.roll(right, (256 - at - 8 * f) % 128, 1)
            high = pltpu.roll(left, (256 - at - 8 * f - 8) % 128, 1)
            e1[f, p] = jnp.where(use_right, low, jnp.where(use_left, high, 0.0))

    def x_low(v):
        return pltpu.roll(v, 1, 0)

    def x_high(v):
        return pltpu.roll(v, v.shape[0] - 1, 0)

    def y_low(v0, v1):
        a0, a1 = pltpu.roll(v0, 1, 1), pltpu.roll(v1, 1, 1)
        return jnp.where(lane == 0, a1, a0), jnp.where(lane == 0, a0, a1)

    def y_high(v0, v1):
        a0, a1 = pltpu.roll(v0, 127, 1), pltpu.roll(v1, 127, 1)
        return jnp.where(lane == 127, a1, a0), jnp.where(lane == 127, a0, a1)

    center, coeffs = chebyshev_table(0.5, FINE_SWEEPS)
    fz0[1] = guarded(e0[0, 1] + e0[0, 0])
    fz1[1] = guarded(e1[0, 1] + e1[0, 0])

    @pl.loop(1, EZ - 1)
    def _(p):
        d0, d1 = e0[0, p], e1[0, p]
        up0, up1 = guarded(d0 + e0[0, p + 1]), guarded(d1 + e1[0, p + 1])
        fz0[p + 1], fz1[p + 1] = up0, up1
        w0, w1 = guarded(d0 + x_low(d0)), guarded(d1 + x_low(d1))
        fx0[p], fx1[p] = w0, w1
        l0, l1 = y_low(d0, d1)
        v0, v1 = guarded(d0 + l0), guarded(d1 + l1)
        fy0[p], fy1[p] = v0, v1
        h0, h1 = y_high(v0, v1)
        g0 = fz0[p] + up0 + w0 + x_high(w0) + v0 + h0
        g1 = fz1[p] + up1 + w1 + x_high(w1) + v1 + h1
        i0 = jnp.where(d0 > 0.0, 1.0 / g0, 0.0)
        i1 = jnp.where(d1 > 0.0, 1.0 / g1, 0.0)
        ig0[p], ig1[p] = i0, i1
        s0[p] = e0[1, p] * i0 * center
        s1[p] = e1[1, p] * i1 * center

    dot_kw = dict(preferred_element_type=jnp.float32, precision=lax.Precision.HIGHEST)
    from_lane = lax.broadcasted_iota(jnp.int32, (128, 128), 0)
    to_lane = lax.broadcasted_iota(jnp.int32, (128, 128), 1)
    pairs = jnp.where(from_lane // 2 == to_lane, 1.0, 0.0).astype(jnp.float32)
    evens = jnp.where(from_lane == 2 * to_lane, 1.0, 0.0).astype(jnp.float32)
    both = evens + jnp.where((from_lane == 2 * to_lane + 2) & (to_lane < CY), 1.0, 0.0).astype(jnp.float32)

    def row_pairs(ref, p):
        return ref[p, pl.ds(X0, CX, stride=2), :] + ref[p, pl.ds(X0 + 1, CX, stride=2), :]

    @pl.loop(0, CZ)
    def _(c):
        p = HZ + 2 * c
        rows = pl.ds(pl.multiple_of(c * CX, CX), CX)
        low_z, high_z = row_pairs(fz0, p), row_pairs(fz0, p + 2)
        low_x = fx0[p, pl.ds(X0, CX, stride=2), :] + fx0[p + 1, pl.ds(X0, CX, stride=2), :]
        high_x = fx0[p, pl.ds(X0 + 2, CX, stride=2), :] + fx0[p + 1, pl.ds(X0 + 2, CX, stride=2), :]
        stage[0, rows] = low_z
        stage[1, rows] = low_x
        stage[2, rows] = low_z + high_z + low_x + high_x
        stage[3, rows] = row_pairs(fy0, p) + row_pairs(fy0, p + 1)
        stage[4, rows] = row_pairs(fy1, p) + row_pairs(fy1, p + 1)

    wide = lanes_of(CZ * CX)
    last = jnp.where(wide == CY - 1, pltpu.roll(stage[4], CY - 1, 1), 0.0)
    total = jnp.dot(stage[2], pairs, **dot_kw) + jnp.dot(stage[3], both, **dot_kw) + last
    whole = (
        total,
        jnp.dot(stage[0], pairs, **dot_kw),
        jnp.dot(stage[1], pairs, **dot_kw),
        jnp.dot(stage[3], evens, **dot_kw),
    )
    for f in range(4):
        ys[f] = (whole[f] * 0.0625).reshape(CZ, CX, 128)

    start_y, wait_y = exchange(3, 2, (ys.at[pl.ds(0, 4)],) * 2, (yr.at[0, pl.ds(0, 4)], yr.at[1, pl.ds(0, 4)]))
    start_y()

    def sweep(k):
        first, last_plane = 2 + k, EZ - 2 - k
        keep, push = coeffs[k]

        def step(p, carry):
            c0, c1, f0, f1 = carry
            n0, n1 = s0[p + 1], s1[p + 1]
            g0 = fz0[p + 1] * (n0 - c0)
            g1 = fz1[p + 1] * (n1 - c1)
            a0 = fx0[p] * (c0 - x_low(c0))
            a1 = fx1[p] * (c1 - x_low(c1))
            l0, l1 = y_low(c0, c1)
            b0 = fy0[p] * (c0 - l0)
            b1 = fy1[p] * (c1 - l1)
            h0, h1 = y_high(b0, b1)
            r0 = e0[1, p] - ((f0 - g0) + (a0 - x_high(a0)) + (b0 - h0))
            r1 = e1[1, p] - ((f1 - g1) + (a1 - x_high(a1)) + (b1 - h1))
            e0[1, p] = r0
            mine = c0[X0:X0 + BX]
            xs[p] = mine if k == 0 else xs[p] + mine
            if k + 1 < FINE_SWEEPS:
                e1[1, p] = r1
                s0[p] = keep * c0 + push * (r0 * ig0[p])
                s1[p] = keep * c1 + push * (r1 * ig1[p])
            return n0, n1, g0, g1

        c0, c1 = s0[first], s1[first]
        lax.fori_loop(
            first, last_plane, step,
            (c0, c1, fz0[first] * (c0 - s0[first - 1]), fz1[first] * (c1 - s1[first - 1])),
        )

    clane = lanes_of(CX)

    def merge(f, target):
        @pl.loop(0, CZ)
        def _(z):
            right = jnp.where(there[2][1], pltpu.roll(yr[0, f, z], 64, 1), 0.0)
            left = jnp.where(there[2][0], pltpu.roll(yr[1, f, z], 64, 1), 0.0)
            target[8 + z, 8:8 + CX] = jnp.where(
                clane < CY, ys[f, z], jnp.where(clane < 96, right, left)
            )

    sweep(0)
    sweep(1)
    wait_y()
    for f in range(4):
        merge(f, cs.at[f])
    start_x, wait_x = exchange(
        4, 1,
        (cs.at[:, pl.ds(8, CZ), pl.ds(8, 8)], cs.at[:, pl.ds(8, CZ), pl.ds(16, 8)]),
        (cs.at[:, pl.ds(8, CZ), pl.ds(24, 8)], cs.at[:, pl.ds(8, CZ), pl.ds(0, 8)]),
    )
    start_x()
    sweep(2)
    sweep(3)

    @pl.loop(0, CZ)
    def _(c):
        p = HZ + 2 * c
        rows = pl.ds(pl.multiple_of(c * CX, CX), CX)
        stage[0, rows] = row_pairs(e0.at[1], p) + row_pairs(e0.at[1], p + 1)

    ys[4] = (jnp.dot(stage[0], pairs, **dot_kw) * 0.125).reshape(CZ, CX, 128)
    start_y, wait_y = exchange(5, 2, (ys.at[4],) * 2, (yr.at[0, 4], yr.at[1, 4]))
    start_y()
    wait_x()
    start_z, wait_z = exchange(
        6, 0,
        (cs.at[:, pl.ds(8, 8)], cs.at[:, pl.ds(8, 8)]),
        (cs.at[:, pl.ds(16, 8)], cs.at[:, pl.ds(0, 8)]),
    )
    start_z()
    wait_y()
    merge(4, cr)
    start_x, wait_x = exchange(
        7, 1,
        (cr.at[pl.ds(8, CZ), pl.ds(8, 8)], cr.at[pl.ds(8, CZ), pl.ds(16, 8)]),
        (cr.at[pl.ds(8, CZ), pl.ds(24, 8)], cr.at[pl.ds(8, CZ), pl.ds(0, 8)]),
    )
    start_x()
    wait_x()
    start_r, wait_r = exchange(
        8, 0, (cr.at[pl.ds(8, 8)], cr.at[pl.ds(8, 8)]), (cr.at[pl.ds(16, 8)], cr.at[pl.ds(0, 8)])
    )
    start_r()
    wait_z()
    wait_r()

    center, ccoeffs = chebyshev_table(0.1, COARSE_SWEEPS)

    @pl.loop(1, KZ - 1)
    def _(p):
        diagonal = cs[0, p]
        inverse = jnp.where(diagonal > 0.0, 1.0 / diagonal, 0.0)
        csx[0, p] = inverse
        csx[1, p] = cr[p] * inverse * center

    def coarse_sweep(k):
        first, last_plane = 2 + k, KZ - 2 - k
        keep, push = ccoeffs[k]

        def step(p, carry):
            below, here = carry
            above = csx[1, p + 1]
            fx, fy = cs[2, p], cs[3, p]
            summed = cs[1, p] * below + cs[1, p + 1] * above
            summed = summed + fx * x_low(here) + x_high(fx * here)
            summed = summed + fy * pltpu.roll(here, 1, 1) + pltpu.roll(fy * here, 127, 1)
            r = cr[p] - (cs[0, p] * here - summed)
            cr[p] = r
            csx[1, p] = keep * here + push * (r * csx[0, p])
            return here, above

        lax.fori_loop(first, last_plane, step, (csx[1, first - 1], csx[1, first]))

    for k in range(COARSE_SWEEPS):
        @pl.loop(0, CZ)
        def _(z):
            mine = csx[1, 8 + z, 8:8 + CX]
            cx[z] = mine if k == 0 else cx[z] + mine
        if k + 1 < COARSE_SWEEPS:
            coarse_sweep(k)

    spread = jnp.where(to_lane // 2 == from_lane, 1.0, 0.0).astype(jnp.float32)
    stage[1] = jnp.dot(cx[...].reshape(CZ * CX, 128), spread, **dot_kw)

    @pl.loop(0, CZ)
    def _(c):
        coarse_ref[c, 0] = cx[c, :, 0:CY]
        wide_rows = stage[1, pl.ds(pl.multiple_of(c * CX, CX), CX), :]
        stage[2, pl.ds(0, CX, stride=2), :] = wide_rows
        stage[2, pl.ds(1, CX, stride=2), :] = wide_rows
        twice = stage[2, 0:BX, :]
        for i in (0, 1):
            out_ref[2 * c + i, 0] = xs[HZ + 2 * c + i] + twice


def body(right_side, phase, density_scale):
    fine = pltpu.VMEM((EZ, EX, 128), jnp.float32)
    return pl.pallas_call(
        kernel,
        out_shape=(
            jax.ShapeDtypeStruct((NZ, 1, BX, BY), jnp.float32),
            jax.ShapeDtypeStruct((CZ, 1, CX, CY), jnp.float32),
        ),
        in_specs=[pl.BlockSpec(memory_space=pltpu.VMEM)] * 3,
        out_specs=(pl.BlockSpec(memory_space=pltpu.VMEM),) * 2,
        scratch_shapes=[
            pltpu.VMEM((2, EZ, EX, 128), jnp.float32),
            pltpu.VMEM((2, EZ, EX, 128), jnp.float32),
            *([fine] * 10),
            pltpu.VMEM((EZ, BX, 128), jnp.float32),
            pltpu.VMEM((2, 9, NZ, 128), jnp.float32),
            pltpu.VMEM((2, 9, NZ, 128), jnp.float32),
            pltpu.VMEM((2, 4, EX, 128), jnp.float32),
            pltpu.VMEM((2, 4, EX, 128), jnp.float32),
            pltpu.VMEM((5, CZ * CX, 128), jnp.float32),
            pltpu.VMEM((4, KZ, KX, 128), jnp.float32),
            pltpu.VMEM((KZ, KX, 128), jnp.float32),
            pltpu.VMEM((2, KZ, KX, 128), jnp.float32),
            pltpu.VMEM((5, CZ, CX, 128), jnp.float32),
            pltpu.VMEM((2, 5, CZ, CX, 128), jnp.float32),
            pltpu.VMEM((CZ, CX, 128), jnp.float32),
            pltpu.SemaphoreType.DMA((18,)),
            pltpu.SemaphoreType.DMA((18,)),
        ],
        compiler_params=pltpu.CompilerParams(
            collective_id=0, has_side_effects=True, vmem_limit_bytes=40 << 20
        ),
        name="vcycle",
    )(right_side, phase, density_scale)


def solution(mesh):
    placed = P("gz", "xy", None, None)
    return jax.shard_map(
        body,
        mesh=mesh,
        in_specs=(placed, placed, placed),
        out_specs=(placed, placed),
        check_vma=False,
    )
```

time: 443 us -> 92.8 us (0.21)
  the two profiles are of different devices: /device:TPU:38 before, /device:TPU:104 now
where the time goes in v1:
time: 92.8 us; the launch traced here: 92.6 us
  Pallas kernels  87.7 us (95%)
  local copies, waits for them, and re-layouts  4.18 us (5%)
    pallas_call x1, Pallas kernels, body(): pl.pallas_call(kernel, out_shape=(jax.ShapeDtypeStruct((NZ, 1, BX, BY), j...  87.7 us
    unnamed x8, local copies, waits for them, and re-layouts  4.18 us

profile of v1, /device:TPU:104, one launch (start us, length us, event | category | flops | bytes accessed | tf_op | source)
XLA Modules:
  0.0 92.6 jit_solution(784441005884625457)
XLA Ops:
  0.6 0.0 copy-start
  0.6 0.9 %copy-done = f32[16,1,32,128]{3,2,1,0:T(8,128)S(1)} copy-done((f32[16,1,32,128]{3,2,1,0:T(8,128)S(1)}, f32[16,1,32,128]{3,2,1,0:T(8,128)}, u32[]{:S(2)}) %copy-start) | copy-done | bytes 262168
  1.6 0.0 copy-start.1
  1.6 0.9 %copy-done.1 = s32[16,1,32,128]{3,2,1,0:T(8,128)S(1)} copy-done((s32[16,1,32,128]{3,2,1,0:T(8,128)S(1)}, s32[16,1,32,128]{3,2,1,0:T(8,128)}, u32[]{:S(2)}) %copy-start.1) | copy-done | bytes 262168
  2.5 0.0 copy-start.2
  2.5 0.9 %copy-done.2 = f32[16,1,32,128]{3,2,1,0:T(8,128)S(1)} copy-done((f32[16,1,32,128]{3,2,1,0:T(8,128)S(1)}, f32[16,1,32,128]{3,2,1,0:T(8,128)}, u32[]{:S(2)}) %copy-start.2) | copy-done | bytes 262168
  3.5 87.7 %vcycle.1 = (f32[16,1,32,128]{3,2,1,0:T(8,128)S(1)}, f32[8,1,16,64]{3,2,1,0:T(8,128)S(1)}) custom-call(f32[16,1,32,128]{3,2,1,0:T(8,128)S(1)} %copy-done, s32[16,1,32,128]{3,2,1,0:T(8,128)S(1)} %copy-done.1, f32[16,1,32,128]{3,2,1,0:T(8,128)S(1)} %copy-done.2), custom_call_target="tpu_custom_call" | custom-call | tf_op jit(solution)/shard_map/vcycle/pallas_call | solution.py:386
  91.2 0.7 copy.7
  91.9 0.6 copy.8
Async XLA Ops:
  0.6 1.0 %copy-start = (f32[16,1,32,128]{3,2,1,0:T(8,128)S(1)}, f32[16,1,32,128]{3,2,1,0:T(8,128)}, u32[]{:S(2)}) copy-start(f32[16,1,32,128]{3,2,1,0:T(8,128)} %right_ref.1) | copy-start | bytes 786436
  1.6 0.9 %copy-start.1 = (s32[16,1,32,128]{3,2,1,0:T(8,128)S(1)}, s32[16,1,32,128]{3,2,1,0:T(8,128)}, u32[]{:S(2)}) copy-start(s32[16,1,32,128]{3,2,1,0:T(8,128)} %phase_ref.1) | copy-start | bytes 786436
  2.5 0.9 %copy-start.2 = (f32[16,1,32,128]{3,2,1,0:T(8,128)S(1)}, f32[16,1,32,128]{3,2,1,0:T(8,128)}, u32[]{:S(2)}) copy-start(f32[16,1,32,128]{3,2,1,0:T(8,128)} %scale_ref.1) | copy-start | bytes 786436

commit v2 on v1

v2 whole, which is shorter than its diff:
```python
import jax
import jax.numpy as jnp
from jax import lax
from jax.experimental import pallas as pl
from jax.experimental.pallas import tpu as pltpu
from jax.sharding import PartitionSpec as P

PY = 8
FINE_SWEEPS = 4
COARSE_SWEEPS = 8

NZ, BX, BY = 16, 32, 128
HZ = 5
EZ, EX = NZ + 2 * HZ, BX + 16
X0 = 8
CZ, CX, CY = 8, 16, 64
KZ, KX = CZ + 16, CX + 16


def chebyshev_table(low_bound, sweeps):
    middle = 0.5 * (2.0 + low_bound)
    radius = 0.5 * (2.0 - low_bound)
    quotient = middle / radius
    previous = 1.0 / quotient
    coeffs = []
    for number in range(sweeps):
        current = 1.0 / (2.0 * quotient - previous)
        coeffs.append((current * previous, 2.0 * current / radius))
        previous = current
    return (1.0 / middle, coeffs)


def lanes_of(rows):
    return lax.broadcasted_iota(jnp.int32, (rows, 128), 1)


def face(total):
    return 2.0 / jnp.maximum(total, 1e-3)


def kernel(
    right_ref, phase_ref, scale_ref, out_ref, coarse_ref,
    e0, e1, s0, s1, r0, r1, fz0, fz1, fx0, fx1, fy0, fy1, gy0, gy1, ig0, ig1,
    xsend, xrecv, pack, unpack, stage,
    cs, cr, ci, sx, rx, ys, yr, cx,
    send_sem, recv_sem,
):
    b = lax.axis_index("xy")
    g = lax.axis_index("gz")
    row, col = b // PY, b % PY
    n_rows = lax.axis_size("xy") // PY
    n_gz = lax.axis_size("gz")
    there = ((g > 0, g < n_gz - 1), (row > 0, row < n_rows - 1), (col > 0, col < PY - 1))

    def neighbour(axis, side):
        by = 1 if side else -1
        if axis == 0:
            return {"xy": b, "gz": g + by}
        return {"xy": b + by * (PY if axis == 1 else 1), "gz": g}

    def exchange(number, axis, sources, targets):
        copies = []
        for side in (0, 1):
            index = 2 * number + side
            copies.append(
                pltpu.make_async_remote_copy(
                    src_ref=sources[side], dst_ref=targets[side],
                    send_sem=send_sem.at[index], recv_sem=recv_sem.at[index],
                    device_id=neighbour(axis, side), device_id_type=pl.DeviceIdType.MESH,
                )
            )

        def start():
            for side in (0, 1):
                pl.when(there[axis][side])(copies[side].start)

        def wait():
            for side in (0, 1):
                pl.when(there[axis][1 - side])(copies[side].wait_recv)
            for side in (0, 1):
                pl.when(there[axis][side])(copies[side].wait_send)

        return start, wait

    for f in (0, 1):
        for p in range(EZ):
            if HZ <= p < HZ + NZ:
                e0[f, p, 0:X0] = jnp.zeros((X0, 128), jnp.float32)
                e0[f, p, X0 + BX:EX] = jnp.zeros((EX - X0 - BX, 128), jnp.float32)
            else:
                e0[f, p] = jnp.zeros((EX, 128), jnp.float32)

    barrier = pltpu.get_barrier_semaphore()
    count = jnp.int32(0)
    for axis in (0, 1, 2):
        for side in (0, 1):
            count = count + there[axis][side].astype(jnp.int32)

            @pl.when(there[axis][side])
            def _():
                pl.semaphore_signal(
                    barrier, inc=1, device_id=neighbour(axis, side),
                    device_id_type=pl.DeviceIdType.MESH,
                )

    for z in range(NZ):
        heavy = jnp.where(phase_ref[z, 0] == 1, 1000.0, 1.0).astype(jnp.float32)
        e0[0, HZ + z, X0:X0 + BX] = heavy * scale_ref[z, 0]
        e0[1, HZ + z, X0:X0 + BX] = right_ref[z, 0]

    @pl.loop(0, KZ)
    def _(p):
        for f in range(4):
            cs[f, p] = jnp.zeros((KX + 8, 128), jnp.float32)
        cr[p] = jnp.zeros((KX + 8, 128), jnp.float32)

    for j in range(9):
        f, at = (0, j) if j < 5 else (1, j - 5)
        width = 5 - f
        xsend[0, j] = e0[f, HZ:HZ + NZ, X0 + at, :]
        xsend[1, j] = e0[f, HZ:HZ + NZ, X0 + BX - width + at, :]

    pl.semaphore_wait(barrier, count)

    start, wait = exchange(0, 1, (xsend.at[0], xsend.at[1]), (xrecv.at[0], xrecv.at[1]))
    start()
    wait()
    for side in (0, 1):
        @pl.when(there[1][1 - side])
        def _():
            for j in range(9):
                f, at = (0, j) if j < 5 else (1, j - 5)
                width = 5 - f
                to = X0 + BX + at if side == 0 else X0 - width + at
                e0[f, HZ:HZ + NZ, to, :] = xrecv[side, j]

    start, wait = exchange(
        1, 0,
        (e0.at[:, pl.ds(HZ, HZ)], e0.at[:, pl.ds(NZ, HZ)]),
        (e0.at[:, pl.ds(HZ + NZ, HZ)], e0.at[:, pl.ds(0, HZ)]),
    )
    start()
    wait()

    lane = lanes_of(EX)

    for a in range(4):
        packed = [None, None]
        for i in range(min(8, EZ - 8 * a)):
            for f in (0, 1):
                v = e0[f, 8 * a + i]
                at = 16 * i + 8 * f
                for side in (0, 1):
                    rolled = pltpu.roll(v, (at + 8 * side) % 128, 1)
                    packed[side] = rolled if packed[side] is None else jnp.where(lane < at, packed[side], rolled)
        pack[0, a], pack[1, a] = packed

    start, wait = exchange(2, 2, (pack.at[0], pack.at[1]), (unpack.at[0], unpack.at[1]))
    start()
    wait()

    use_right = (lane < 8) & there[2][1]
    use_left = (lane >= 120) & there[2][0]
    for a in range(4):
        right, left = unpack[0, a], unpack[1, a]
        for i in range(min(8, EZ - 8 * a)):
            for f in (0, 1):
                at = 16 * i + 8 * f
                low = pltpu.roll(right, (128 - at) % 128, 1)
                high = pltpu.roll(left, (120 - at) % 128, 1)
                e1[f, 8 * a + i] = jnp.where(use_right, low, jnp.where(use_left, high, 0.0))

    lane8 = lanes_of(8)

    def y_low(v):
        a0, a1 = pltpu.roll(v[0], 1, 1), pltpu.roll(v[1], 1, 1)
        return jnp.where(lane8 == 0, a1, a0), jnp.where(lane8 == 0, a0, a1)

    def y_high(v):
        a0, a1 = pltpu.roll(v[0], 127, 1), pltpu.roll(v[1], 127, 1)
        return jnp.where(lane8 == 127, a1, a0), jnp.where(lane8 == 127, a0, a1)

    center, coeffs = chebyshev_table(0.5, FINE_SWEEPS)
    es, fzs, fxs, fys, gys, igs = (e0, e1), (fz0, fz1), (fx0, fx1), (fy0, fy1), (gy0, gy1), (ig0, ig1)

    def at_rows(refs, p, r, *lead):
        return [ref[(*lead, p, pl.ds(r, 8))] for ref in refs]

    tiles = [4 + 8 * i for i in range(5)]

    def faces_step(p, below):
        out = []
        for i, r in enumerate(tiles):
            d = at_rows(es, p, r, 0)
            above = at_rows(es, p + 1, r, 0)
            before = at_rows(es, p, r - 1, 0)
            after = at_rows(es, p, r + 1, 0)
            left, right = y_low(d), y_high(d)
            for t in (0, 1):
                up = face(d[t] + above[t])
                w, e = face(d[t] + before[t]), face(d[t] + after[t])
                v, h = face(d[t] + left[t]), face(d[t] + right[t])
                inverse = jnp.where(d[t] > 0.0, 1.0 / (below[2 * i + t] + up + w + e + v + h), 0.0)
                fzs[t][p + 1, pl.ds(r, 8)] = up
                fxs[t][p, pl.ds(r, 8)] = w
                if r == tiles[-1]:
                    fxs[t][p, pl.ds(r + 1, 8)] = e
                fys[t][p, pl.ds(r, 8)] = v
                gys[t][p, pl.ds(r, 8)] = h
                igs[t][p, pl.ds(r, 8)] = inverse
                ss[t][0, p, pl.ds(r, 8)] = es[t][1, p, pl.ds(r, 8)] * inverse * center
                out.append(up)
        return tuple(out)

    ss, rs = (s0, s1), (r0, r1)
    below = []
    for r in tiles:
        d, above = at_rows(es, 0, r, 0), at_rows(es, 1, r, 0)
        for t in (0, 1):
            up = face(d[t] + above[t])
            fzs[t][1, pl.ds(r, 8)] = up
            below.append(up)
    lax.fori_loop(1, EZ - 1, faces_step, tuple(below))

    dot_kw = dict(preferred_element_type=jnp.float32, precision=lax.Precision.HIGHEST)
    from_lane = lax.broadcasted_iota(jnp.int32, (128, 128), 0)
    to_lane = lax.broadcasted_iota(jnp.int32, (128, 128), 1)
    pairs = jnp.where(from_lane // 2 == to_lane, 1.0, 0.0).astype(jnp.float32)
    evens = jnp.where(from_lane == 2 * to_lane, 1.0, 0.0).astype(jnp.float32)
    both = evens + jnp.where((from_lane == 2 * to_lane + 2) & (to_lane < CY), 1.0, 0.0).astype(jnp.float32)

    def row_pairs(ref, p):
        return ref[p, pl.ds(X0, CX, stride=2), :] + ref[p, pl.ds(X0 + 1, CX, stride=2), :]

    for c in range(CZ):
        p = HZ + 2 * c
        rows = pl.ds(c * CX, CX)
        low_z, high_z = row_pairs(fz0, p), row_pairs(fz0, p + 2)
        low_x = fx0[p, pl.ds(X0, CX, stride=2), :] + fx0[p + 1, pl.ds(X0, CX, stride=2), :]
        high_x = fx0[p, pl.ds(X0 + 2, CX, stride=2), :] + fx0[p + 1, pl.ds(X0 + 2, CX, stride=2), :]
        stage[0, rows] = low_z
        stage[1, rows] = low_x
        stage[2, rows] = low_z + high_z + low_x + high_x
        stage[3, rows] = row_pairs(fy0, p) + row_pairs(fy0, p + 1)
        stage[4, rows] = row_pairs(fy1, p) + row_pairs(fy1, p + 1)

    wide = lanes_of(CZ * CX)
    last = jnp.where(wide == CY - 1, pltpu.roll(stage[4], CY - 1, 1), 0.0)
    total = jnp.dot(stage[2], pairs, **dot_kw) + jnp.dot(stage[3], both, **dot_kw) + last
    whole = (
        total,
        jnp.dot(stage[0], pairs, **dot_kw),
        jnp.dot(stage[1], pairs, **dot_kw),
        jnp.dot(stage[3], evens, **dot_kw),
    )
    for f in range(4):
        ys[f] = (whole[f] * 0.0625).reshape(CZ, CX, 128)

    start_y, wait_y = exchange(3, 2, (ys.at[pl.ds(0, 4)],) * 2, (yr.at[0, pl.ds(0, 4)], yr.at[1, pl.ds(0, 4)]))
    start_y()

    def sweep(k):
        first, end = 2 + k, EZ - 2 - k
        keep, push = coeffs[k]
        rows_of = tiles if k + 1 < FINE_SWEEPS else [X0 + 8 * i for i in range(4)]
        lanes = (0, 1) if k + 1 < FINE_SWEEPS else (0,)
        source = (lambda t, p, r: es[t][1, p, pl.ds(r, 8)]) if k == 0 else (lambda t, p, r: rs[t][k - 1, p, pl.ds(r, 8)])

        def step(j, fluxes):
            fluxes = list(fluxes)
            for i, r in enumerate(rows_of):
                for u in (0, 1):
                    p = first + 2 * j + u
                    c = at_rows(ss, p, r, k)
                    left, right = y_low(c), y_high(c)
                    for t in lanes:
                        up = fzs[t][p + 1, pl.ds(r, 8)] * (ss[t][k, p + 1, pl.ds(r, 8)] - c[t])
                        total = fluxes[len(lanes) * i + t] - up
                        total = total + fxs[t][p, pl.ds(r, 8)] * (c[t] - ss[t][k, p, pl.ds(r - 1, 8)])
                        total = total + fxs[t][p, pl.ds(r + 1, 8)] * (c[t] - ss[t][k, p, pl.ds(r + 1, 8)])
                        total = total + fys[t][p, pl.ds(r, 8)] * (c[t] - left[t])
                        total = total + gys[t][p, pl.ds(r, 8)] * (c[t] - right[t])
                        residual = source(t, p, r) - total
                        rs[t][k, p, pl.ds(r, 8)] = residual
                        if k + 1 < FINE_SWEEPS:
                            ss[t][k + 1, p, pl.ds(r, 8)] = keep * c[t] + (push * residual) * igs[t][p, pl.ds(r, 8)]
                        fluxes[len(lanes) * i + t] = up
            return tuple(fluxes)

        fluxes = []
        for r in rows_of:
            for t in lanes:
                fluxes.append(
                    fzs[t][first, pl.ds(r, 8)] * (ss[t][k, first, pl.ds(r, 8)] - ss[t][k, first - 1, pl.ds(r, 8)])
                )
        lax.fori_loop(0, (end - first) // 2, step, tuple(fluxes))

    clane = lanes_of(CX)

    def merge(f, target):
        for z in range(CZ):
            right = jnp.where(there[2][1], pltpu.roll(yr[0, f, z], 64, 1), 0.0)
            left = jnp.where(there[2][0], pltpu.roll(yr[1, f, z], 64, 1), 0.0)
            target[8 + z, 8:8 + CX] = jnp.where(
                clane < CY, ys[f, z], jnp.where(clane < 96, right, left)
            )

    sweep(0)
    sweep(1)
    wait_y()
    for f in range(4):
        merge(f, cs.at[f])
    start_x, wait_x = exchange(
        4, 1,
        (cs.at[:, pl.ds(8, CZ), pl.ds(8, 8)], cs.at[:, pl.ds(8, CZ), pl.ds(16, 8)]),
        (cs.at[:, pl.ds(8, CZ), pl.ds(24, 8)], cs.at[:, pl.ds(8, CZ), pl.ds(0, 8)]),
    )
    start_x()
    sweep(2)
    sweep(3)

    last_residual = rs[0].at[FINE_SWEEPS - 1]
    for c in range(CZ):
        p = HZ + 2 * c
        stage[0, pl.ds(c * CX, CX)] = row_pairs(last_residual, p) + row_pairs(last_residual, p + 1)

    ys[4] = (jnp.dot(stage[0], pairs, **dot_kw) * 0.125).reshape(CZ, CX, 128)
    start_y, wait_y = exchange(5, 2, (ys.at[4],) * 2, (yr.at[0, 4], yr.at[1, 4]))
    start_y()
    wait_x()
    start_z, wait_z = exchange(
        6, 0,
        (cs.at[:, pl.ds(8, 8), pl.ds(0, KX)], cs.at[:, pl.ds(8, 8), pl.ds(0, KX)]),
        (cs.at[:, pl.ds(16, 8), pl.ds(0, KX)], cs.at[:, pl.ds(0, 8), pl.ds(0, KX)]),
    )
    start_z()
    wait_y()
    merge(4, cr)
    start_x, wait_x = exchange(
        7, 1,
        (cr.at[pl.ds(8, CZ), pl.ds(8, 8)], cr.at[pl.ds(8, CZ), pl.ds(16, 8)]),
        (cr.at[pl.ds(8, CZ), pl.ds(24, 8)], cr.at[pl.ds(8, CZ), pl.ds(0, 8)]),
    )
    start_x()
    wait_x()
    start_r, wait_r = exchange(
        8, 0, (cr.at[pl.ds(8, 8), pl.ds(0, KX)], cr.at[pl.ds(8, 8), pl.ds(0, KX)]), (cr.at[pl.ds(16, 8), pl.ds(0, KX)], cr.at[pl.ds(0, 8), pl.ds(0, KX)])
    )
    start_r()
    wait_z()
    wait_r()

    center, ccoeffs = chebyshev_table(0.1, COARSE_SWEEPS)

    for p in range(1, KZ - 1):
        diagonal = cs[0, p, 0:KX]
        inverse = jnp.where(diagonal > 0.0, 1.0 / diagonal, 0.0)
        ci[p, 0:KX] = inverse
        sx[0, p, 0:KX] = cr[p, 0:KX] * inverse * center

    def coarse_sweep(k):
        halo = COARSE_SWEEPS - 2 - k
        first, count = 8 - halo, CZ + 2 * halo
        n_tiles = (CX + 2 * halo + 7) // 8
        r_first = min(8 - halo, KX + 7 - 8 * n_tiles)
        rows_of = [r_first + 8 * i for i in range(n_tiles)]
        keep, push = ccoeffs[k]
        unroll = 4 if count % 4 == 0 else 2

        def step(j, fluxes):
            fluxes = list(fluxes)
            for i, r in enumerate(rows_of):
                rows = pl.ds(r, 8)
                for u in range(unroll):
                    p = first + unroll * j + u
                    c = sx[k, p, rows]
                    above = sx[k, p + 1, rows]
                    fz = cs[1, p + 1, rows]
                    fy = cs[3, p, rows]
                    total = cs[0, p, rows] * c - fluxes[i] - fz * above
                    total = total - cs[2, p, rows] * sx[k, p, pl.ds(r - 1, 8)]
                    total = total - cs[2, p, pl.ds(r + 1, 8)] * sx[k, p, pl.ds(r + 1, 8)]
                    total = total - fy * pltpu.roll(c, 1, 1) - pltpu.roll(fy * c, 127, 1)
                    residual = (cr if k == 0 else rx.at[k])[p, rows] - total
                    if k + 2 < COARSE_SWEEPS:
                        rx[k + 1, p, rows] = residual
                    sx[k + 1, p, rows] = keep * c + (push * residual) * ci[p, rows]
                    fluxes[i] = fz * c
            return tuple(fluxes)

        lax.fori_loop(
            0, count // unroll, step,
            tuple(cs[1, first, pl.ds(r, 8)] * sx[k, first - 1, pl.ds(r, 8)] for r in rows_of),
        )

    for k in range(COARSE_SWEEPS - 1):
        coarse_sweep(k)
    for z in range(CZ):
        mine = sx[0, 8 + z, 8:8 + CX]
        for k in range(1, COARSE_SWEEPS):
            mine = mine + sx[k, 8 + z, 8:8 + CX]
        cx[z] = mine

    spread = jnp.where(to_lane // 2 == from_lane, 1.0, 0.0).astype(jnp.float32)
    stage[1] = jnp.dot(cx[...].reshape(CZ * CX, 128), spread, **dot_kw)

    for c in range(CZ):
        coarse_ref[c, 0] = cx[c, :, 0:CY]
        wide_rows = stage[1, pl.ds(c * CX, CX), :]
        spot = pl.ds(BX * (c % 2), CX, stride=2), pl.ds(BX * (c % 2) + 1, CX, stride=2)
        stage[2, spot[0], :] = wide_rows
        stage[2, spot[1], :] = wide_rows
        twice = stage[2, pl.ds(BX * (c % 2), BX), :]
        for i in (0, 1):
            mine = s0[0, HZ + 2 * c + i, X0:X0 + BX]
            for k in range(1, FINE_SWEEPS):
                mine = mine + s0[k, HZ + 2 * c + i, X0:X0 + BX]
            out_ref[2 * c + i, 0] = mine + twice


def body(right_side, phase, density_scale):
    fine = pltpu.VMEM((EZ, EX, 128), jnp.float32)
    return pl.pallas_call(
        kernel,
        out_shape=(
            jax.ShapeDtypeStruct((NZ, 1, BX, BY), jnp.float32),
            jax.ShapeDtypeStruct((CZ, 1, CX, CY), jnp.float32),
        ),
        in_specs=[pl.BlockSpec(memory_space=pltpu.VMEM)] * 3,
        out_specs=(pl.BlockSpec(memory_space=pltpu.VMEM),) * 2,
        scratch_shapes=[
            pltpu.VMEM((2, EZ, EX, 128), jnp.float32),
            pltpu.VMEM((2, EZ, EX, 128), jnp.float32),
            *([pltpu.VMEM((FINE_SWEEPS, EZ, EX, 128), jnp.float32)] * 4),
            *([fine] * 10),
            pltpu.VMEM((2, 9, NZ, 128), jnp.float32),
            pltpu.VMEM((2, 9, NZ, 128), jnp.float32),
            pltpu.VMEM((2, 4, EX, 128), jnp.float32),
            pltpu.VMEM((2, 4, EX, 128), jnp.float32),
            pltpu.VMEM((5, CZ * CX, 128), jnp.float32),
            pltpu.VMEM((4, KZ, KX + 8, 128), jnp.float32),
            pltpu.VMEM((KZ, KX + 8, 128), jnp.float32),
            pltpu.VMEM((KZ, KX + 8, 128), jnp.float32),
            pltpu.VMEM((COARSE_SWEEPS, KZ, KX + 8, 128), jnp.float32),
            pltpu.VMEM((COARSE_SWEEPS, KZ, KX + 8, 128), jnp.float32),
            pltpu.VMEM((5, CZ, CX, 128), jnp.float32),
            pltpu.VMEM((2, 5, CZ, CX, 128), jnp.float32),
            pltpu.VMEM((CZ, CX, 128), jnp.float32),
            pltpu.SemaphoreType.DMA((18,)),
            pltpu.SemaphoreType.DMA((18,)),
        ],
        compiler_params=pltpu.CompilerParams(
            collective_id=0, has_side_effects=True, vmem_limit_bytes=40 << 20
        ),
        name="vcycle",
    )(right_side, phase, density_scale)


def solution(mesh):
    placed = P("gz", "xy", None, None)
    return jax.shard_map(
        body,
        mesh=mesh,
        in_specs=(placed, placed, placed),
        out_specs=(placed, placed),
        check_vma=False,
    )
```

time: 92.8 us -> 78.2 us (0.84)
  the two profiles are of different devices: /device:TPU:104 before, /device:TPU:137 now
where the time goes in v2:
time: 78.2 us; the launch traced here: 78 us
  Pallas kernels  73.1 us (93%)
  local copies, waits for them, and re-layouts  4.18 us (5%)
    pallas_call x1, Pallas kernels, body(): pl.pallas_call(kernel, out_shape=(jax.ShapeDtypeStruct((NZ, 1, BX, BY), j...  73.1 us
    unnamed x8, local copies, waits for them, and re-layouts  4.18 us

profile of v2, /device:TPU:137, one launch (start us, length us, event | category | flops | bytes accessed | tf_op | source)
XLA Modules:
  0.0 78.0 jit_solution(8580545356385853807)
XLA Ops:
  0.6 0.0 copy-start
  0.6 0.9 %copy-done = f32[16,1,32,128]{3,2,1,0:T(8,128)S(1)} copy-done((f32[16,1,32,128]{3,2,1,0:T(8,128)S(1)}, f32[16,1,32,128]{3,2,1,0:T(8,128)}, u32[]{:S(2)}) %copy-start) | copy-done | bytes 262168
  1.6 0.0 copy-start.1
  1.6 0.9 %copy-done.1 = s32[16,1,32,128]{3,2,1,0:T(8,128)S(1)} copy-done((s32[16,1,32,128]{3,2,1,0:T(8,128)S(1)}, s32[16,1,32,128]{3,2,1,0:T(8,128)}, u32[]{:S(2)}) %copy-start.1) | copy-done | bytes 262168
  2.5 0.0 copy-start.2
  2.5 0.9 %copy-done.2 = f32[16,1,32,128]{3,2,1,0:T(8,128)S(1)} copy-done((f32[16,1,32,128]{3,2,1,0:T(8,128)S(1)}, f32[16,1,32,128]{3,2,1,0:T(8,128)}, u32[]{:S(2)}) %copy-start.2) | copy-done | bytes 262168
  3.5 73.1 %vcycle.1 = (f32[16,1,32,128]{3,2,1,0:T(8,128)S(1)}, f32[8,1,16,64]{3,2,1,0:T(8,128)S(1)}) custom-call(f32[16,1,32,128]{3,2,1,0:T(8,128)S(1)} %copy-done, s32[16,1,32,128]{3,2,1,0:T(8,128)S(1)} %copy-done.1, f32[16,1,32,128]{3,2,1,0:T(8,128)S(1)} %copy-done.2), custom_call_target="tpu_custom_call" | custom-call | tf_op jit(solution)/shard_map/vcycle/pallas_call | solution.py:423
  76.6 0.7 copy.7
  77.3 0.6 copy.8
Async XLA Ops:
  0.6 1.0 %copy-start = (f32[16,1,32,128]{3,2,1,0:T(8,128)S(1)}, f32[16,1,32,128]{3,2,1,0:T(8,128)}, u32[]{:S(2)}) copy-start(f32[16,1,32,128]{3,2,1,0:T(8,128)} %right_ref.1) | copy-start | bytes 786436
  1.6 0.9 %copy-start.1 = (s32[16,1,32,128]{3,2,1,0:T(8,128)S(1)}, s32[16,1,32,128]{3,2,1,0:T(8,128)}, u32[]{:S(2)}) copy-start(s32[16,1,32,128]{3,2,1,0:T(8,128)} %phase_ref.1) | copy-start | bytes 786436
  2.5 0.9 %copy-start.2 = (f32[16,1,32,128]{3,2,1,0:T(8,128)S(1)}, f32[16,1,32,128]{3,2,1,0:T(8,128)}, u32[]{:S(2)}) copy-start(f32[16,1,32,128]{3,2,1,0:T(8,128)} %scale_ref.1) | copy-start | bytes 786436

commit v3 on v2

--- a/solution.py
+++ b/solution.py
@@ -15,6 +15,9 @@
 X0 = 8
 CZ, CX, CY = 8, 16, 64
 KZ, KX = CZ + 16, CX + 16
+AROUND = [(z, x, y) for z in (-1, 0, 1) for x in (-1, 0, 1) for y in (-1, 0, 1) if z or x or y]
+EDGES = [(-1, -1), (-1, 1), (1, -1), (1, 1)]
+EDGE_ROWS = [(f, j, i) for f in (0, 1) for j in range(1, 5) for i in range(1, 6 - f - j)]
 
 
 def chebyshev_table(low_bound, sweeps):
@@ -41,8 +44,8 @@
 def kernel(
     right_ref, phase_ref, scale_ref, out_ref, coarse_ref,
     e0, e1, s0, s1, r0, r1, fz0, fz1, fx0, fx1, fy0, fy1, gy0, gy1, ig0, ig1,
-    xsend, xrecv, pack, unpack, stage,
-    cs, cr, ci, sx, rx, ys, yr, cx,
+    xsend, xrecv, esend, erecv, pack, unpack, stage,
+    cp, cpack, cps, crp, rpack, crs, cs, cr, ci, sx, rx, cx,
     send_sem, recv_sem,
 ):
     b = lax.axis_index("xy")
@@ -52,35 +55,29 @@
     n_gz = lax.axis_size("gz")
     there = ((g > 0, g < n_gz - 1), (row > 0, row < n_rows - 1), (col > 0, col < PY - 1))
 
-    def neighbour(axis, side):
-        by = 1 if side else -1
-        if axis == 0:
-            return {"xy": b, "gz": g + by}
-        return {"xy": b + by * (PY if axis == 1 else 1), "gz": g}
-
-    def exchange(number, axis, sources, targets):
-        copies = []
-        for side in (0, 1):
-            index = 2 * number + side
-            copies.append(
-                pltpu.make_async_remote_copy(
-                    src_ref=sources[side], dst_ref=targets[side],
-                    send_sem=send_sem.at[index], recv_sem=recv_sem.at[index],
-                    device_id=neighbour(axis, side), device_id_type=pl.DeviceIdType.MESH,
-                )
-            )
-
-        def start():
-            for side in (0, 1):
-                pl.when(there[axis][side])(copies[side].start)
-
-        def wait():
-            for side in (0, 1):
-                pl.when(there[axis][1 - side])(copies[side].wait_recv)
-            for side in (0, 1):
-                pl.when(there[axis][side])(copies[side].wait_send)
-
-        return start, wait
+    def exists(d):
+        found = None
+        for axis in (0, 1, 2):
+            if d[axis]:
+                flag = there[axis][1 if d[axis] > 0 else 0]
+                found = flag if found is None else found & flag
+        return found
+
+    def device(d):
+        return {"xy": b + PY * d[1] + d[2], "gz": g + d[0]}
+
+    sent = []
+
+    def message(number, d, source, target):
+        copy = pltpu.make_async_remote_copy(
+            src_ref=source, dst_ref=target,
+            send_sem=send_sem.at[number], recv_sem=recv_sem.at[number],
+            device_id=device(d), device_id_type=pl.DeviceIdType.MESH,
+        )
+        back = tuple(-v for v in d)
+        sent.append((d, copy))
+        pl.when(exists(d))(copy.start)
+        return lambda: pl.when(exists(back))(copy.wait_recv)
 
     for f in (0, 1):
         for p in range(EZ):
@@ -89,30 +86,34 @@
                 e0[f, p, X0 + BX:EX] = jnp.zeros((EX - X0 - BX, 128), jnp.float32)
             else:
                 e0[f, p] = jnp.zeros((EX, 128), jnp.float32)
+    for side in (0, 1):
+        for a in range(4):
+            unpack[side, a] = jnp.zeros((EX, 128), jnp.float32)
 
     barrier = pltpu.get_barrier_semaphore()
     count = jnp.int32(0)
-    for axis in (0, 1, 2):
-        for side in (0, 1):
-            count = count + there[axis][side].astype(jnp.int32)
-
-            @pl.when(there[axis][side])
-            def _():
-                pl.semaphore_signal(
-                    barrier, inc=1, device_id=neighbour(axis, side),
-                    device_id_type=pl.DeviceIdType.MESH,
-                )
+    for d in AROUND:
+        count = count + exists(d).astype(jnp.int32)
+
+        @pl.when(exists(d))
+        def _():
+            pl.semaphore_signal(barrier, inc=1, device_id=device(d), device_id_type=pl.DeviceIdType.MESH)
 
     for z in range(NZ):
         heavy = jnp.where(phase_ref[z, 0] == 1, 1000.0, 1.0).astype(jnp.float32)
         e0[0, HZ + z, X0:X0 + BX] = heavy * scale_ref[z, 0]
         e0[1, HZ + z, X0:X0 + BX] = right_ref[z, 0]
 
-    @pl.loop(0, KZ)
-    def _(p):
-        for f in range(4):
-            cs[f, p] = jnp.zeros((KX + 8, 128), jnp.float32)
-        cr[p] = jnp.zeros((KX + 8, 128), jnp.float32)
+    for p in range(KZ):
+        for f in (0, 1):
+            cp[f, p] = jnp.zeros((KX, 128), jnp.float32)
+        for side in (0, 1):
+            if p < 6:
+                cps[side, p] = jnp.zeros((KX, 128), jnp.float32)
+            if p < 3:
+                crs[side, p] = jnp.zeros((KX, 128), jnp.float32)
+        if p < 12:
+            crp[p] = jnp.zeros((KX, 128), jnp.float32)
 
     for j in range(9):
         f, at = (0, j) if j < 5 else (1, j - 5)
@@ -120,11 +121,51 @@
         xsend[0, j] = e0[f, HZ:HZ + NZ, X0 + at, :]
         xsend[1, j] = e0[f, HZ:HZ + NZ, X0 + BX - width + at, :]
 
+    for q, (dz, dx) in enumerate(EDGES):
+        for n, (f, j, i) in enumerate(EDGE_ROWS):
+            p = HZ + NZ - j if dz > 0 else HZ + j - 1
+            r = X0 + BX - i if dx > 0 else X0 + i - 1
+            esend[q, n:n + 1] = e0[f, p, r:r + 1, :]
+
+    lane = lanes_of(BX)
+
+    for a in (0, 1):
+        packed = [None, None]
+        for i in range(8):
+            for f in (0, 1):
+                v = e0[f, HZ + 8 * a + i, X0:X0 + BX]
+                at = 16 * i + 8 * f
+                for side in (0, 1):
+                    rolled = pltpu.roll(v, (at + 8 * side) % 128, 1)
+                    packed[side] = rolled if packed[side] is None else jnp.where(lane < at, packed[side], rolled)
+        pack[0, a], pack[1, a] = packed
+
     pl.semaphore_wait(barrier, count)
 
-    start, wait = exchange(0, 1, (xsend.at[0], xsend.at[1]), (xrecv.at[0], xrecv.at[1]))
-    start()
-    wait()
+    waits = []
+    order = sorted(range(26), key=lambda n: (-abs(AROUND[n][1]), abs(AROUND[n][0]) + abs(AROUND[n][2])))
+    for n in order:
+        d = dz, dx, dy = AROUND[n]
+        if dy:
+            side = (dy + 1) // 2
+            size = 1 if dz else 2
+            from_group, to_group = {1: (1, 0), -1: (0, 3), 0: (0, 1)}[dz]
+            from_row, rows = {1: (BX - 8, 8), -1: (0, 8), 0: (0, BX)}[dx]
+            to_row = {1: 0, -1: X0 + BX, 0: X0}[dx]
+            source = pack.at[side, pl.ds(from_group, size), pl.ds(from_row, rows)]
+            target = unpack.at[side, pl.ds(to_group, size), pl.ds(to_row, rows)]
+        elif dz and dx:
+            q = EDGES.index((dz, dx))
+            source, target = esend.at[q], erecv.at[q]
+        elif dx:
+            source, target = xsend.at[(dx + 1) // 2], xrecv.at[(dx + 1) // 2]
+        else:
+            source = e0.at[:, pl.ds(NZ if dz > 0 else HZ, HZ), pl.ds(X0, BX)]
+            target = e0.at[:, pl.ds(0 if dz > 0 else HZ + NZ, HZ), pl.ds(X0, BX)]
+        waits.append(message(n, d, source, target))
+    for wait in waits:
+        wait()
+
     for side in (0, 1):
         @pl.when(there[1][1 - side])
         def _():
@@ -134,41 +175,26 @@
                 to = X0 + BX + at if side == 0 else X0 - width + at
                 e0[f, HZ:HZ + NZ, to, :] = xrecv[side, j]
 
-    start, wait = exchange(
-        1, 0,
-        (e0.at[:, pl.ds(HZ, HZ)], e0.at[:, pl.ds(NZ, HZ)]),
-        (e0.at[:, pl.ds(HZ + NZ, HZ)], e0.at[:, pl.ds(0, HZ)]),
-    )
-    start()
-    wait()
+    for q, (dz, dx) in enumerate(EDGES):
+        @pl.when(exists((-dz, -dx, 0)))
+        def _():
+            for n, (f, j, i) in enumerate(EDGE_ROWS):
+                p = HZ - j if dz > 0 else HZ + NZ + j - 1
+                r = X0 - i if dx > 0 else X0 + BX + i - 1
+                e0[f, p, r:r + 1, :] = erecv[q, n:n + 1]
 
     lane = lanes_of(EX)
-
-    for a in range(4):
-        packed = [None, None]
-        for i in range(min(8, EZ - 8 * a)):
-            for f in (0, 1):
-                v = e0[f, 8 * a + i]
-                at = 16 * i + 8 * f
-                for side in (0, 1):
-                    rolled = pltpu.roll(v, (at + 8 * side) % 128, 1)
-                    packed[side] = rolled if packed[side] is None else jnp.where(lane < at, packed[side], rolled)
-        pack[0, a], pack[1, a] = packed
-
-    start, wait = exchange(2, 2, (pack.at[0], pack.at[1]), (unpack.at[0], unpack.at[1]))
-    start()
-    wait()
-
-    use_right = (lane < 8) & there[2][1]
-    use_left = (lane >= 120) & there[2][0]
     for a in range(4):
         right, left = unpack[0, a], unpack[1, a]
-        for i in range(min(8, EZ - 8 * a)):
+        for i in range(8):
+            p = i - 3 if a == 0 else HZ + 8 * (a - 1) + i
+            if not 0 <= p < EZ:
+                continue
             for f in (0, 1):
                 at = 16 * i + 8 * f
                 low = pltpu.roll(right, (128 - at) % 128, 1)
                 high = pltpu.roll(left, (120 - at) % 128, 1)
-                e1[f, 8 * a + i] = jnp.where(use_right, low, jnp.where(use_left, high, 0.0))
+                e1[f, p] = jnp.where(lane < 8, low, jnp.where(lane >= 120, high, 0.0))
 
     lane8 = lanes_of(8)
 
@@ -225,9 +251,12 @@
     dot_kw = dict(preferred_element_type=jnp.float32, precision=lax.Precision.HIGHEST)
     from_lane = lax.broadcasted_iota(jnp.int32, (128, 128), 0)
     to_lane = lax.broadcasted_iota(jnp.int32, (128, 128), 1)
-    pairs = jnp.where(from_lane // 2 == to_lane, 1.0, 0.0).astype(jnp.float32)
-    evens = jnp.where(from_lane == 2 * to_lane, 1.0, 0.0).astype(jnp.float32)
-    both = evens + jnp.where((from_lane == 2 * to_lane + 2) & (to_lane < CY), 1.0, 0.0).astype(jnp.float32)
+    def ones(mask):
+        return jnp.where(mask, 1.0, 0.0).astype(jnp.float32)
+
+    pairs = (ones(from_lane // 2 == to_lane), ones(from_lane // 2 == to_lane - CY))
+    evens = (ones(from_lane == 2 * to_lane), ones(from_lane == 2 * to_lane - 2 * CY))
+    both = evens[0] + jnp.where((from_lane == 2 * to_lane + 2) & (to_lane < CY), 1.0, 0.0).astype(jnp.float32)
 
     def row_pairs(ref, p):
         return ref[p, pl.ds(X0, CX, stride=2), :] + ref[p, pl.ds(X0 + 1, CX, stride=2), :]
@@ -246,18 +275,42 @@
 
     wide = lanes_of(CZ * CX)
     last = jnp.where(wide == CY - 1, pltpu.roll(stage[4], CY - 1, 1), 0.0)
-    total = jnp.dot(stage[2], pairs, **dot_kw) + jnp.dot(stage[3], both, **dot_kw) + last
-    whole = (
-        total,
-        jnp.dot(stage[0], pairs, **dot_kw),
-        jnp.dot(stage[1], pairs, **dot_kw),
-        jnp.dot(stage[3], evens, **dot_kw),
-    )
-    for f in range(4):
-        ys[f] = (whole[f] * 0.0625).reshape(CZ, CX, 128)
-
-    start_y, wait_y = exchange(3, 2, (ys.at[pl.ds(0, 4)],) * 2, (yr.at[0, pl.ds(0, 4)], yr.at[1, pl.ds(0, 4)]))
-    start_y()
+    first_pair = jnp.dot(stage[2], pairs[0], **dot_kw) + jnp.dot(stage[3], both, **dot_kw) + last
+    first_pair = first_pair + jnp.dot(stage[0], pairs[1], **dot_kw)
+    second_pair = jnp.dot(stage[1], pairs[0], **dot_kw) + jnp.dot(stage[3], evens[1], **dot_kw)
+    fields = [(v * 0.0625).reshape(CZ, CX, 128) for v in (first_pair, second_pair)]
+    cp[0, 8:8 + CZ, 8:8 + CX], cp[1, 8:8 + CZ, 8:8 + CX] = fields
+    clane = lanes_of(CX)
+    for a in (0, 1):
+        packed = [None, None]
+        for i in range(4):
+            for f in range(4):
+                at = 32 * i + 8 * f
+                for side in (0, 1):
+                    shift = (at - 64 * (f % 2) - 56 * side) % 128
+                    rolled = pltpu.roll(fields[f // 2][4 * a + i], shift, 1)
+                    packed[side] = rolled if packed[side] is None else jnp.where(clane < at, packed[side], rolled)
+        cpack[0, a], cpack[1, a] = packed
+
+    def coarse_messages(number, depth, array, strips_from, strips_to):
+        lead = (slice(None),) if len(array.shape) == 4 else ()
+        groups = strips_from.shape[1]
+        waits = []
+        for n in order:
+            d = dz, dx, dy = AROUND[n]
+            from_row, to_row, rows = {1: (8, 0, 8), -1: (0, 24, 8), 0: (0, 8, CX)}[dx]
+            block = {1: 0, -1: 2, 0: 1}[dz]
+            if dy:
+                side = (dy + 1) // 2
+                source = strips_from.at[side, :, pl.ds(from_row, rows)]
+                target = strips_to.at[side, pl.ds(groups * block, groups), pl.ds(to_row, rows)]
+            else:
+                source = array.at[(*lead, pl.ds(depth, depth), pl.ds(8 + from_row, rows))]
+                target = array.at[(*lead, pl.ds(depth * block, depth), pl.ds(to_row, rows))]
+            waits.append(message(number + n, d, source, target))
+        return waits
+
+    face_waits = coarse_messages(26, CZ, cp, cpack, cps)
 
     def sweep(k):
         first, end = 2 + k, EZ - 2 - k
@@ -295,68 +348,51 @@
                 )
         lax.fori_loop(0, (end - first) // 2, step, tuple(fluxes))
 
-    clane = lanes_of(CX)
-
-    def merge(f, target):
-        for z in range(CZ):
-            right = jnp.where(there[2][1], pltpu.roll(yr[0, f, z], 64, 1), 0.0)
-            left = jnp.where(there[2][0], pltpu.roll(yr[1, f, z], 64, 1), 0.0)
-            target[8 + z, 8:8 + CX] = jnp.where(
-                clane < CY, ys[f, z], jnp.where(clane < 96, right, left)
-            )
-
-    sweep(0)
-    sweep(1)
-    wait_y()
-    for f in range(4):
-        merge(f, cs.at[f])
-    start_x, wait_x = exchange(
-        4, 1,
-        (cs.at[:, pl.ds(8, CZ), pl.ds(8, 8)], cs.at[:, pl.ds(8, CZ), pl.ds(16, 8)]),
-        (cs.at[:, pl.ds(8, CZ), pl.ds(24, 8)], cs.at[:, pl.ds(8, CZ), pl.ds(0, 8)]),
-    )
-    start_x()
-    sweep(2)
-    sweep(3)
+    for k in range(FINE_SWEEPS):
+        sweep(k)
 
     last_residual = rs[0].at[FINE_SWEEPS - 1]
     for c in range(CZ):
         p = HZ + 2 * c
         stage[0, pl.ds(c * CX, CX)] = row_pairs(last_residual, p) + row_pairs(last_residual, p + 1)
-
-    ys[4] = (jnp.dot(stage[0], pairs, **dot_kw) * 0.125).reshape(CZ, CX, 128)
-    start_y, wait_y = exchange(5, 2, (ys.at[4],) * 2, (yr.at[0, 4], yr.at[1, 4]))
-    start_y()
-    wait_x()
-    start_z, wait_z = exchange(
-        6, 0,
-        (cs.at[:, pl.ds(8, 8), pl.ds(0, KX)], cs.at[:, pl.ds(8, 8), pl.ds(0, KX)]),
-        (cs.at[:, pl.ds(16, 8), pl.ds(0, KX)], cs.at[:, pl.ds(0, 8), pl.ds(0, KX)]),
-    )
-    start_z()
-    wait_y()
-    merge(4, cr)
-    start_x, wait_x = exchange(
-        7, 1,
-        (cr.at[pl.ds(8, CZ), pl.ds(8, 8)], cr.at[pl.ds(8, CZ), pl.ds(16, 8)]),
-        (cr.at[pl.ds(8, CZ), pl.ds(24, 8)], cr.at[pl.ds(8, CZ), pl.ds(0, 8)]),
-    )
-    start_x()
-    wait_x()
-    start_r, wait_r = exchange(
-        8, 0, (cr.at[pl.ds(8, 8), pl.ds(0, KX)], cr.at[pl.ds(8, 8), pl.ds(0, KX)]), (cr.at[pl.ds(16, 8), pl.ds(0, KX)], cr.at[pl.ds(0, 8), pl.ds(0, KX)])
-    )
-    start_r()
-    wait_z()
-    wait_r()
-
+    half = CZ * CX // 2
+    planes = jnp.dot(stage[0, 0:half], pairs[0], **dot_kw) + jnp.dot(stage[0, half:2 * half], pairs[1], **dot_kw)
+    planes = (planes * 0.125).reshape(CZ // 2, CX, 128)
+    crp[4:8, 8:8 + CX] = planes
+    packed = [None, None]
+    for z in range(CZ):
+        for side in (0, 1):
+            rolled = pltpu.roll(planes[z % 4], (8 * z - 64 * (z // 4) - 56 * side) % 128, 1)
+            packed[side] = rolled if packed[side] is None else jnp.where(clane < 8 * z, packed[side], rolled)
+    rpack[0, 0], rpack[1, 0] = packed
+    right_waits = coarse_messages(52, CZ // 2, crp, rpack, crs)
+
+    xlane = lanes_of(KX)
+
+    def widen(base, second, right, left, at):
+        base = pltpu.roll(base, 64, 1) if second else base
+        right = pltpu.roll(right, (64 - at) % 128, 1)
+        left = pltpu.roll(left, (120 - at) % 128, 1)
+        return jnp.where(xlane < CY, base, jnp.where(xlane < 96, right, left))
+
+    for wait in face_waits:
+        wait()
+    for p in range(KZ):
+        for f in range(4):
+            cs[f, p, 0:KX] = widen(
+                cp[f // 2, p], f % 2, cps[0, p // 4], cps[1, p // 4], 32 * (p % 4) + 8 * f
+            )
+        diagonal = cs[0, p, 0:KX]
+        ci[p, 0:KX] = jnp.where(diagonal > 0.0, 1.0 / diagonal, 0.0)
+
+    for wait in right_waits:
+        wait()
     center, ccoeffs = chebyshev_table(0.1, COARSE_SWEEPS)
-
-    for p in range(1, KZ - 1):
-        diagonal = cs[0, p, 0:KX]
-        inverse = jnp.where(diagonal > 0.0, 1.0 / diagonal, 0.0)
-        ci[p, 0:KX] = inverse
-        sx[0, p, 0:KX] = cr[p, 0:KX] * inverse * center
+    for p in range(KZ):
+        z = p % 8
+        value = widen(crp[4 * (p // 8) + z % 4], z // 4, crs[0, p // 8], crs[1, p // 8], 8 * z)
+        cr[p, 0:KX] = value
+        sx[0, p, 0:KX] = value * ci[p, 0:KX] * center
 
     def coarse_sweep(k):
         halo = COARSE_SWEEPS - 2 - k
@@ -399,7 +435,7 @@
         mine = sx[0, 8 + z, 8:8 + CX]
         for k in range(1, COARSE_SWEEPS):
             mine = mine + sx[k, 8 + z, 8:8 + CX]
-        cx[z] = mine
+        cx[z] = jnp.where(clane < CY, mine, 0.0)
 
     spread = jnp.where(to_lane // 2 == from_lane, 1.0, 0.0).astype(jnp.float32)
     stage[1] = jnp.dot(cx[...].reshape(CZ * CX, 128), spread, **dot_kw)
@@ -416,6 +452,9 @@
             for k in range(1, FINE_SWEEPS):
                 mine = mine + s0[k, HZ + 2 * c + i, X0:X0 + BX]
             out_ref[2 * c + i, 0] = mine + twice
+
+    for d, copy in sent:
+        pl.when(exists(d))(copy.wait_send)
 
 
 def body(right_side, phase, density_scale):
@@ -435,19 +474,25 @@
             *([fine] * 10),
             pltpu.VMEM((2, 9, NZ, 128), jnp.float32),
             pltpu.VMEM((2, 9, NZ, 128), jnp.float32),
-            pltpu.VMEM((2, 4, EX, 128), jnp.float32),
+            pltpu.VMEM((4, 16, 128), jnp.float32),
+            pltpu.VMEM((4, 16, 128), jnp.float32),
+            pltpu.VMEM((2, 2, BX, 128), jnp.float32),
             pltpu.VMEM((2, 4, EX, 128), jnp.float32),
             pltpu.VMEM((5, CZ * CX, 128), jnp.float32),
+            pltpu.VMEM((2, KZ, KX, 128), jnp.float32),
+            pltpu.VMEM((2, 2, CX, 128), jnp.float32),
+            pltpu.VMEM((2, 6, KX, 128), jnp.float32),
+            pltpu.VMEM((12, KX, 128), jnp.float32),
+            pltpu.VMEM((2, 1, CX, 128), jnp.float32),
+            pltpu.VMEM((2, 3, KX, 128), jnp.float32),
             pltpu.VMEM((4, KZ, KX + 8, 128), jnp.float32),
             pltpu.VMEM((KZ, KX + 8, 128), jnp.float32),
             pltpu.VMEM((KZ, KX + 8, 128), jnp.float32),
             pltpu.VMEM((COARSE_SWEEPS, KZ, KX + 8, 128), jnp.float32),
             pltpu.VMEM((COARSE_SWEEPS, KZ, KX + 8, 128), jnp.float32),
-            pltpu.VMEM((5, CZ, CX, 128), jnp.float32),
-            pltpu.VMEM((2, 5, CZ, CX, 128), jnp.float32),
             pltpu.VMEM((CZ, CX, 128), jnp.float32),
-            pltpu.SemaphoreType.DMA((18,)),
-            pltpu.SemaphoreType.DMA((18,)),
+            pltpu.SemaphoreType.DMA((78,)),
+            pltpu.SemaphoreType.DMA((78,)),
         ],
         compiler_params=pltpu.CompilerParams(
             collective_id=0, has_side_effects=True, vmem_limit_bytes=40 << 20

time: 78.2 us -> 71 us (0.908)
  the two profiles are of different devices: /device:TPU:137 before, /device:TPU:113 now
where the time goes in v3:
time: 71 us; the launch traced here: 70.8 us
  Pallas kernels  65.9 us (93%)
  local copies, waits for them, and re-layouts  4.18 us (6%)
    pallas_call x1, Pallas kernels, body(): pl.pallas_call(kernel, out_shape=(jax.ShapeDtypeStruct((NZ, 1, BX, BY), j...  65.9 us
    unnamed x8, local copies, waits for them, and re-layouts  4.18 us

profile of v3, /device:TPU:113, one launch (start us, length us, event | category | flops | bytes accessed | tf_op | source)
XLA Modules:
  0.0 70.8 jit_solution(7750170531858816382)
XLA Ops:
  0.6 0.0 copy-start
  0.6 0.9 %copy-done = f32[16,1,32,128]{3,2,1,0:T(8,128)S(1)} copy-done((f32[16,1,32,128]{3,2,1,0:T(8,128)S(1)}, f32[16,1,32,128]{3,2,1,0:T(8,128)}, u32[]{:S(2)}) %copy-start) | copy-done | bytes 262168
  1.6 0.0 copy-start.1
  1.6 0.9 %copy-done.1 = s32[16,1,32,128]{3,2,1,0:T(8,128)S(1)} copy-done((s32[16,1,32,128]{3,2,1,0:T(8,128)S(1)}, s32[16,1,32,128]{3,2,1,0:T(8,128)}, u32[]{:S(2)}) %copy-start.1) | copy-done | bytes 262168
  2.5 0.0 copy-start.2
  2.5 0.9 %copy-done.2 = f32[16,1,32,128]{3,2,1,0:T(8,128)S(1)} copy-done((f32[16,1,32,128]{3,2,1,0:T(8,128)S(1)}, f32[16,1,32,128]{3,2,1,0:T(8,128)}, u32[]{:S(2)}) %copy-start.2) | copy-done | bytes 262168
  3.5 65.9 %vcycle.1 = (f32[16,1,32,128]{3,2,1,0:T(8,128)S(1)}, f32[8,1,16,64]{3,2,1,0:T(8,128)S(1)}) custom-call(f32[16,1,32,128]{3,2,1,0:T(8,128)S(1)} %copy-done, s32[16,1,32,128]{3,2,1,0:T(8,128)S(1)} %copy-done.1, f32[16,1,32,128]{3,2,1,0:T(8,128)S(1)} %copy-done.2), custom_call_target="tpu_custom_call" | custom-call | tf_op jit(solution)/shard_map/vcycle/pallas_call | solution.py:462
  69.4 0.7 copy.7
  70.1 0.6 copy.8
Async XLA Ops:
  0.6 1.0 %copy-start = (f32[16,1,32,128]{3,2,1,0:T(8,128)S(1)}, f32[16,1,32,128]{3,2,1,0:T(8,128)}, u32[]{:S(2)}) copy-start(f32[16,1,32,128]{3,2,1,0:T(8,128)} %right_ref.1) | copy-start | bytes 786436
  1.6 0.9 %copy-start.1 = (s32[16,1,32,128]{3,2,1,0:T(8,128)S(1)}, s32[16,1,32,128]{3,2,1,0:T(8,128)}, u32[]{:S(2)}) copy-start(s32[16,1,32,128]{3,2,1,0:T(8,128)} %phase_ref.1) | copy-start | bytes 786436
  2.5 0.9 %copy-start.2 = (f32[16,1,32,128]{3,2,1,0:T(8,128)S(1)}, f32[16,1,32,128]{3,2,1,0:T(8,128)}, u32[]{:S(2)}) copy-start(f32[16,1,32,128]{3,2,1,0:T(8,128)} %scale_ref.1) | copy-start | bytes 786436

commit v4 on v3

--- a/solution.py
+++ b/solution.py
@@ -17,6 +17,7 @@
 KZ, KX = CZ + 16, CX + 16
 AROUND = [(z, x, y) for z in (-1, 0, 1) for x in (-1, 0, 1) for y in (-1, 0, 1) if z or x or y]
 EDGES = [(-1, -1), (-1, 1), (1, -1), (1, 1)]
+X_ROWS = [(0, i) for i in range(5)] + [(1, i) for i in range(4)]
 EDGE_ROWS = [(f, j, i) for f in (0, 1) for j in range(1, 5) for i in range(1, 6 - f - j)]
 
 
@@ -42,11 +43,11 @@
 
 
 def kernel(
-    right_ref, phase_ref, scale_ref, out_ref, coarse_ref,
+    right_ref, phase_ref, scale_ref, out_ref, coarse_ref, phase, scale,
     e0, e1, s0, s1, r0, r1, fz0, fz1, fx0, fx1, fy0, fy1, gy0, gy1, ig0, ig1,
     xsend, xrecv, esend, erecv, pack, unpack, stage,
     cp, cpack, cps, crp, rpack, crs, cs, cr, ci, sx, rx, cx,
-    send_sem, recv_sem,
+    fetch_sem, send_sem, recv_sem,
 ):
     b = lax.axis_index("xy")
     g = lax.axis_index("gz")
@@ -79,17 +80,6 @@
         pl.when(exists(d))(copy.start)
         return lambda: pl.when(exists(back))(copy.wait_recv)
 
-    for f in (0, 1):
-        for p in range(EZ):
-            if HZ <= p < HZ + NZ:
-                e0[f, p, 0:X0] = jnp.zeros((X0, 128), jnp.float32)
-                e0[f, p, X0 + BX:EX] = jnp.zeros((EX - X0 - BX, 128), jnp.float32)
-            else:
-                e0[f, p] = jnp.zeros((EX, 128), jnp.float32)
-    for side in (0, 1):
-        for a in range(4):
-            unpack[side, a] = jnp.zeros((EX, 128), jnp.float32)
-
     barrier = pltpu.get_barrier_semaphore()
     count = jnp.int32(0)
     for d in AROUND:
@@ -99,27 +89,47 @@
         def _():
             pl.semaphore_signal(barrier, inc=1, device_id=device(d), device_id_type=pl.DeviceIdType.MESH)
 
+    fetched = [
+        pltpu.make_async_copy(source, target, fetch_sem.at[n])
+        for n, (source, target) in enumerate((
+            (phase_ref.at[:, 0], phase), (scale_ref.at[:, 0], scale),
+            (right_ref.at[:, 0], e0.at[1, pl.ds(HZ, NZ), pl.ds(X0, BX)]),
+        ))
+    ]
+    for copy in fetched:
+        copy.start()
+
+    def clear(ref, *at):
+        ref[at] = jnp.zeros(ref.at[at].shape, jnp.float32)
+
+    def clear_without(d, ref, *at):
+        @pl.when(jnp.logical_not(exists(d)))
+        def _():
+            clear(ref, *at)
+
+    for f in (0, 1):
+        for p in range(EZ):
+            clear(e0, f, p, slice(0, X0))
+            clear(e0, f, p, slice(X0 + BX, EX))
+            if p < HZ or p >= HZ + NZ:
+                clear_without((-1 if p < HZ else 1, 0, 0), e0, f, p, slice(X0, X0 + BX))
+    for d in AROUND:
+        dz, dx, dy = d
+        if dy:
+            groups = {-1: (0,), 0: (1, 2), 1: (3,)}[dz]
+            rows = {-1: slice(0, X0), 0: slice(X0, X0 + BX), 1: slice(X0 + BX, EX)}[dx]
+            for a in groups:
+                clear_without(d, unpack, 0 if dy > 0 else 1, a, rows)
+
+    for copy in fetched:
+        copy.wait()
     for z in range(NZ):
-        heavy = jnp.where(phase_ref[z, 0] == 1, 1000.0, 1.0).astype(jnp.float32)
-        e0[0, HZ + z, X0:X0 + BX] = heavy * scale_ref[z, 0]
-        e0[1, HZ + z, X0:X0 + BX] = right_ref[z, 0]
-
-    for p in range(KZ):
-        for f in (0, 1):
-            cp[f, p] = jnp.zeros((KX, 128), jnp.float32)
-        for side in (0, 1):
-            if p < 6:
-                cps[side, p] = jnp.zeros((KX, 128), jnp.float32)
-            if p < 3:
-                crs[side, p] = jnp.zeros((KX, 128), jnp.float32)
-        if p < 12:
-            crp[p] = jnp.zeros((KX, 128), jnp.float32)
-
-    for j in range(9):
-        f, at = (0, j) if j < 5 else (1, j - 5)
-        width = 5 - f
-        xsend[0, j] = e0[f, HZ:HZ + NZ, X0 + at, :]
-        xsend[1, j] = e0[f, HZ:HZ + NZ, X0 + BX - width + at, :]
+        heavy = jnp.where(phase[z] == 1, 1000.0, 1.0).astype(jnp.float32)
+        e0[0, HZ + z, X0:X0 + BX] = heavy * scale[z]
+
+    for j, (f, away) in enumerate(X_ROWS):
+        xsend[0, j] = e0[f, HZ:HZ + NZ, X0 + away, :]
+        xsend[1, j] = e0[f, HZ:HZ + NZ, X0 + BX - 1 - away, :]
 
     for q, (dz, dx) in enumerate(EDGES):
         for n, (f, j, i) in enumerate(EDGE_ROWS):
@@ -140,13 +150,38 @@
                     packed[side] = rolled if packed[side] is None else jnp.where(lane < at, packed[side], rolled)
         pack[0, a], pack[1, a] = packed
 
+    for p in range(KZ):
+        for f in (0, 1):
+            clear(cp, f, p)
+        for side in (0, 1):
+            if p < 6:
+                clear(cps, side, p)
+            if p < 3:
+                clear(crs, side, p)
+        if p < 12:
+            clear(crp, p)
+
     pl.semaphore_wait(barrier, count)
 
-    waits = []
+    first_waits, waits = [], []
     order = sorted(range(26), key=lambda n: (-abs(AROUND[n][1]), abs(AROUND[n][0]) + abs(AROUND[n][2])))
     for n in order:
         d = dz, dx, dy = AROUND[n]
-        if dy:
+        if abs(dz) + abs(dx) + abs(dy) > 1:
+            continue
+        if dx:
+            side = (dx + 1) // 2
+            source, target = xsend.at[side, pl.ds(0, 1)], xrecv.at[side, pl.ds(0, 1)]
+        elif dz:
+            source = e0.at[0, HZ + NZ - 1 if dz > 0 else HZ, pl.ds(X0, BX)]
+            target = e0.at[0, HZ - 1 if dz > 0 else HZ + NZ, pl.ds(X0, BX)]
+        else:
+            side = (dy + 1) // 2
+            source, target = pack.at[side], unpack.at[side, pl.ds(1, 2), pl.ds(X0, BX)]
+        first_waits.append(message(n, d, source, target))
+    for n in order:
+        d = dz, dx, dy = AROUND[n]
+        if dy and (dz or dx):
             side = (dy + 1) // 2
             size = 1 if dz else 2
             from_group, to_group = {1: (1, 0), -1: (0, 3), 0: (0, 1)}[dz]
@@ -154,47 +189,50 @@
             to_row = {1: 0, -1: X0 + BX, 0: X0}[dx]
             source = pack.at[side, pl.ds(from_group, size), pl.ds(from_row, rows)]
             target = unpack.at[side, pl.ds(to_group, size), pl.ds(to_row, rows)]
+            waits.append(message(n, d, source, target))
         elif dz and dx:
             q = EDGES.index((dz, dx))
-            source, target = esend.at[q], erecv.at[q]
+            waits.append(message(n, d, esend.at[q], erecv.at[q]))
         elif dx:
-            source, target = xsend.at[(dx + 1) // 2], xrecv.at[(dx + 1) // 2]
-        else:
-            source = e0.at[:, pl.ds(NZ if dz > 0 else HZ, HZ), pl.ds(X0, BX)]
-            target = e0.at[:, pl.ds(0 if dz > 0 else HZ + NZ, HZ), pl.ds(X0, BX)]
-        waits.append(message(n, d, source, target))
-    for wait in waits:
+            side = (dx + 1) // 2
+            waits.append(message(78 + side, d, xsend.at[side, pl.ds(1, 8)], xrecv.at[side, pl.ds(1, 8)]))
+        elif dz:
+            side = (dz + 1) // 2
+            for f in (0, 1):
+                if dz > 0:
+                    source, target = HZ + NZ - 5 + f, f
+                else:
+                    source, target = HZ + 1 - f, HZ + NZ + 1 - f
+                waits.append(message(
+                    80 + 2 * f + side, d,
+                    e0.at[f, pl.ds(source, 4), pl.ds(X0, BX)],
+                    e0.at[f, pl.ds(target, 4), pl.ds(X0, BX)],
+                ))
+
+    def place_rows(numbers):
+        for side in (0, 1):
+            @pl.when(there[1][1 - side])
+            def _():
+                for j in numbers:
+                    f, away = X_ROWS[j]
+                    to = X0 + BX + away if side == 0 else X0 - 1 - away
+                    e0[f, HZ:HZ + NZ, to, :] = xrecv[side, j]
+
+    def unpack_plane(p, rows):
+        a = (p + 3) // 8
+        right, left = unpack[0, a, rows], unpack[1, a, rows]
+        lane = lanes_of(right.shape[0])
+        for f in (0, 1):
+            at = 16 * ((p + 3) % 8) + 8 * f
+            low = pltpu.roll(right, (128 - at) % 128, 1)
+            high = pltpu.roll(left, (120 - at) % 128, 1)
+            e1[f, p, rows] = jnp.where(lane < 8, low, jnp.where(lane >= 120, high, 0.0))
+
+    for wait in first_waits:
         wait()
-
-    for side in (0, 1):
-        @pl.when(there[1][1 - side])
-        def _():
-            for j in range(9):
-                f, at = (0, j) if j < 5 else (1, j - 5)
-                width = 5 - f
-                to = X0 + BX + at if side == 0 else X0 - width + at
-                e0[f, HZ:HZ + NZ, to, :] = xrecv[side, j]
-
-    for q, (dz, dx) in enumerate(EDGES):
-        @pl.when(exists((-dz, -dx, 0)))
-        def _():
-            for n, (f, j, i) in enumerate(EDGE_ROWS):
-                p = HZ - j if dz > 0 else HZ + NZ + j - 1
-                r = X0 - i if dx > 0 else X0 + BX + i - 1
-                e0[f, p, r:r + 1, :] = erecv[q, n:n + 1]
-
-    lane = lanes_of(EX)
-    for a in range(4):
-        right, left = unpack[0, a], unpack[1, a]
-        for i in range(8):
-            p = i - 3 if a == 0 else HZ + 8 * (a - 1) + i
-            if not 0 <= p < EZ:
-                continue
-            for f in (0, 1):
-                at = 16 * i + 8 * f
-                low = pltpu.roll(right, (128 - at) % 128, 1)
-                high = pltpu.roll(left, (120 - at) % 128, 1)
-                e1[f, p] = jnp.where(lane < 8, low, jnp.where(lane >= 120, high, 0.0))
+    place_rows([0])
+    for p in range(HZ, HZ + NZ):
+        unpack_plane(p, slice(X0, X0 + BX))
 
     lane8 = lanes_of(8)
 
@@ -214,22 +252,19 @@
 
     tiles = [4 + 8 * i for i in range(5)]
 
-    def faces_step(p, below):
+    def plane_faces(p, below, rows_of, lanes):
         out = []
-        for i, r in enumerate(tiles):
+        for i, r in enumerate(rows_of):
             d = at_rows(es, p, r, 0)
-            above = at_rows(es, p + 1, r, 0)
-            before = at_rows(es, p, r - 1, 0)
-            after = at_rows(es, p, r + 1, 0)
             left, right = y_low(d), y_high(d)
-            for t in (0, 1):
-                up = face(d[t] + above[t])
-                w, e = face(d[t] + before[t]), face(d[t] + after[t])
+            for k, t in enumerate(lanes):
+                up = face(d[t] + es[t][0, p + 1, pl.ds(r, 8)])
+                w, e = face(d[t] + es[t][0, p, pl.ds(r - 1, 8)]), face(d[t] + es[t][0, p, pl.ds(r + 1, 8)])
                 v, h = face(d[t] + left[t]), face(d[t] + right[t])
-                inverse = jnp.where(d[t] > 0.0, 1.0 / (below[2 * i + t] + up + w + e + v + h), 0.0)
+                inverse = jnp.where(d[t] > 0.0, 1.0 / (below[len(lanes) * i + k] + up + w + e + v + h), 0.0)
                 fzs[t][p + 1, pl.ds(r, 8)] = up
                 fxs[t][p, pl.ds(r, 8)] = w
-                if r == tiles[-1]:
+                if r == rows_of[-1]:
                     fxs[t][p, pl.ds(r + 1, 8)] = e
                 fys[t][p, pl.ds(r, 8)] = v
                 gys[t][p, pl.ds(r, 8)] = h
@@ -238,15 +273,25 @@
                 out.append(up)
         return tuple(out)
 
+    def faces(first, end, rows_of, lanes):
+        below = []
+        for r in rows_of:
+            for t in lanes:
+                up = face(es[t][0, first - 1, pl.ds(r, 8)] + es[t][0, first, pl.ds(r, 8)])
+                fzs[t][first, pl.ds(r, 8)] = up
+                below.append(up)
+        step = 2 if (end - first) % 2 == 0 else 1
+
+        def some(j, below):
+            for u in range(step):
+                below = plane_faces(first + step * j + u, below, rows_of, lanes)
+            return below
+
+        lax.fori_loop(0, (end - first) // step, some, tuple(below))
+
     ss, rs = (s0, s1), (r0, r1)
-    below = []
-    for r in tiles:
-        d, above = at_rows(es, 0, r, 0), at_rows(es, 1, r, 0)
-        for t in (0, 1):
-            up = face(d[t] + above[t])
-            fzs[t][1, pl.ds(r, 8)] = up
-            below.append(up)
-    lax.fori_loop(1, EZ - 1, faces_step, tuple(below))
+    own_rows = [X0 + 8 * i for i in range(4)]
+    faces(HZ, HZ + NZ, own_rows, (0,))
 
     dot_kw = dict(preferred_element_type=jnp.float32, precision=lax.Precision.HIGHEST)
     from_lane = lax.broadcasted_iota(jnp.int32, (128, 128), 0)
@@ -256,7 +301,7 @@
 
     pairs = (ones(from_lane // 2 == to_lane), ones(from_lane // 2 == to_lane - CY))
     evens = (ones(from_lane == 2 * to_lane), ones(from_lane == 2 * to_lane - 2 * CY))
-    both = evens[0] + jnp.where((from_lane == 2 * to_lane + 2) & (to_lane < CY), 1.0, 0.0).astype(jnp.float32)
+    odds = ones(from_lane == 2 * to_lane + 1)
 
     def row_pairs(ref, p):
         return ref[p, pl.ds(X0, CX, stride=2), :] + ref[p, pl.ds(X0 + 1, CX, stride=2), :]
@@ -271,11 +316,10 @@
         stage[1, rows] = low_x
         stage[2, rows] = low_z + high_z + low_x + high_x
         stage[3, rows] = row_pairs(fy0, p) + row_pairs(fy0, p + 1)
-        stage[4, rows] = row_pairs(fy1, p) + row_pairs(fy1, p + 1)
-
-    wide = lanes_of(CZ * CX)
-    last = jnp.where(wide == CY - 1, pltpu.roll(stage[4], CY - 1, 1), 0.0)
-    first_pair = jnp.dot(stage[2], pairs[0], **dot_kw) + jnp.dot(stage[3], both, **dot_kw) + last
+        stage[4, rows] = row_pairs(gy0, p) + row_pairs(gy0, p + 1)
+
+    first_pair = jnp.dot(stage[2], pairs[0], **dot_kw) + jnp.dot(stage[3], evens[0], **dot_kw)
+    first_pair = first_pair + jnp.dot(stage[4], odds, **dot_kw)
     first_pair = first_pair + jnp.dot(stage[0], pairs[1], **dot_kw)
     second_pair = jnp.dot(stage[1], pairs[0], **dot_kw) + jnp.dot(stage[3], evens[1], **dot_kw)
     fields = [(v * 0.0625).reshape(CZ, CX, 128) for v in (first_pair, second_pair)]
@@ -310,7 +354,56 @@
             waits.append(message(number + n, d, source, target))
         return waits
 
-    face_waits = coarse_messages(26, CZ, cp, cpack, cps)
+    def along(number, axis, source_of, target_of):
+        waits = []
+        for side in (0, 1):
+            d = tuple((2 * side - 1) if k == axis else 0 for k in range(3))
+            waits.append(message(number + side, d, source_of(side), target_of(side)))
+        return waits
+
+    edge, halo = (8, 16), (24, 0)
+    planes_own, groups_own = pl.ds(8, CZ), pl.ds(2, 2)
+    y_waits = along(
+        26, 2, lambda side: cpack.at[side], lambda side: cps.at[side, groups_own, pl.ds(8, CX)]
+    )
+    x_waits = along(
+        28, 1, lambda side: cp.at[:, planes_own, pl.ds(edge[side], 8)],
+        lambda side: cp.at[:, planes_own, pl.ds(halo[side], 8)],
+    )
+    face_waits = along(
+        30, 0, lambda side: cp.at[:, planes_own, pl.ds(8, CX)],
+        lambda side: cp.at[:, pl.ds((16, 0)[side], CZ), pl.ds(8, CX)],
+    )
+    for wait in y_waits:
+        wait()
+    x_waits += along(
+        32, 1, lambda side: cps.at[:, groups_own, pl.ds(edge[side], 8)],
+        lambda side: cps.at[:, groups_own, pl.ds(halo[side], 8)],
+    )
+
+
+    for wait in waits:
+        wait()
+    place_rows(range(1, 9))
+    for q, (dz, dx) in enumerate(EDGES):
+        @pl.when(exists((-dz, -dx, 0)))
+        def _():
+            for n, (f, j, i) in enumerate(EDGE_ROWS):
+                p = HZ - j if dz > 0 else HZ + NZ + j - 1
+                r = X0 - i if dx > 0 else X0 + BX + i - 1
+                e0[f, p, r:r + 1, :] = erecv[q, n:n + 1]
+
+    for p in range(EZ):
+        if HZ <= p < HZ + NZ:
+            unpack_plane(p, slice(0, X0))
+            unpack_plane(p, slice(X0 + BX, EX))
+        else:
+            unpack_plane(p, slice(0, EX))
+    faces(HZ, HZ + NZ, [4], (0,))
+    faces(HZ, HZ + NZ, [36], (0,))
+    faces(HZ, HZ + NZ, tiles, (1,))
+    faces(1, HZ, tiles, (0, 1))
+    faces(HZ + NZ, EZ - 1, tiles, (0, 1))
 
     def sweep(k):
         first, end = 2 + k, EZ - 2 - k
@@ -348,8 +441,20 @@
                 )
         lax.fori_loop(0, (end - first) // 2, step, tuple(fluxes))
 
-    for k in range(FINE_SWEEPS):
-        sweep(k)
+    sweep(0)
+    sweep(1)
+    sweep(2)
+    for wait in x_waits:
+        wait()
+    for n, r in ((34, 0), (36, 24)):
+        face_waits += along(
+            n, 0, lambda side: cp.at[:, planes_own, pl.ds(r, 8)],
+            lambda side: cp.at[:, pl.ds((16, 0)[side], CZ), pl.ds(r, 8)],
+        )
+    face_waits += along(
+        38, 0, lambda side: cps.at[:, groups_own], lambda side: cps.at[:, pl.ds((4, 0)[side], 2)]
+    )
+    sweep(3)
 
     last_residual = rs[0].at[FINE_SWEEPS - 1]
     for c in range(CZ):
@@ -465,9 +570,11 @@
             jax.ShapeDtypeStruct((NZ, 1, BX, BY), jnp.float32),
             jax.ShapeDtypeStruct((CZ, 1, CX, CY), jnp.float32),
         ),
-        in_specs=[pl.BlockSpec(memory_space=pltpu.VMEM)] * 3,
+        in_specs=[pl.BlockSpec(memory_space=pltpu.HBM)] * 3,
         out_specs=(pl.BlockSpec(memory_space=pltpu.VMEM),) * 2,
         scratch_shapes=[
+            pltpu.VMEM((NZ, BX, BY), jnp.int32),
+            pltpu.VMEM((NZ, BX, BY), jnp.float32),
             pltpu.VMEM((2, EZ, EX, 128), jnp.float32),
             pltpu.VMEM((2, EZ, EX, 128), jnp.float32),
             *([pltpu.VMEM((FINE_SWEEPS, EZ, EX, 128), jnp.float32)] * 4),
@@ -491,11 +598,12 @@
             pltpu.VMEM((COARSE_SWEEPS, KZ, KX + 8, 128), jnp.float32),
             pltpu.VMEM((COARSE_SWEEPS, KZ, KX + 8, 128), jnp.float32),
             pltpu.VMEM((CZ, CX, 128), jnp.float32),
-            pltpu.SemaphoreType.DMA((78,)),
-            pltpu.SemaphoreType.DMA((78,)),
+            pltpu.SemaphoreType.DMA((3,)),
+            pltpu.SemaphoreType.DMA((84,)),
+            pltpu.SemaphoreType.DMA((84,)),
         ],
         compiler_params=pltpu.CompilerParams(
-            collective_id=0, has_side_effects=True, vmem_limit_bytes=40 << 20
+            collective_id=0, has_side_effects=True, vmem_limit_bytes=107 << 19
         ),
         name="vcycle",
     )(right_side, phase, density_scale)

time: 71 us -> 56.1 us (0.79)
  Pallas kernels: 65.9 us -> 54 us
  local copies, waits for them, and re-layouts: 4.18 us -> 1.33 us
    pallas_call x1, Pallas kernels: 65.9 us -> 54 us  [body(): pl.pallas_call(kernel, out_shape=(jax.ShapeDtypeStruct((NZ, 1, BX, BY), j...]
    unnamed x8 -> x2, local copies, waits for them, and re-layouts: 4.18 us -> 1.33 us
where the time goes in v4:
time: 56.1 us; the launch traced here: 56 us
  Pallas kernels  54 us (96%)
  local copies, waits for them, and re-layouts  1.33 us (2%)
  between operations  0.64 us (1%)
    pallas_call x1, Pallas kernels, body(): pl.pallas_call(kernel, out_shape=(jax.ShapeDtypeStruct((NZ, 1, BX, BY), j...  54 us
    unnamed x2, local copies, waits for them, and re-layouts  1.33 us

profile of v4, /device:TPU:113, one launch (start us, length us, event | category | flops | bytes accessed | tf_op | source)
XLA Modules:
  0.0 56.0 jit_solution(2008971145469051482)
XLA Ops:
  0.6 54.0 %vcycle.1 = (f32[16,1,32,128]{3,2,1,0:T(8,128)S(1)}, f32[8,1,16,64]{3,2,1,0:T(8,128)S(1)}) custom-call(f32[16,1,32,128]{3,2,1,0:T(8,128)} %right_ref.1, s32[16,1,32,128]{3,2,1,0:T(8,128)} %phase_ref.1, f32[16,1,32,128]{3,2,1,0:T(8,128)} %scale_ref.1), custom_call_target="tpu_custom_call" | custom-call | tf_op jit(solution)/shard_map/vcycle/pallas_call | solution.py:567
  54.7 0.7 %copy.7 = f32[16,1,32,128]{3,2,1,0:T(8,128)} copy(f32[16,1,32,128]{3,2,1,0:T(8,128)S(1)} %get-tuple-element.4) | data formatting | bytes 524288
  55.4 0.6 %copy.8 = f32[8,1,16,64]{3,2,1,0:T(8,128)} copy(f32[8,1,16,64]{3,2,1,0:T(8,128)S(1)} %get-tuple-element.5) | data formatting | bytes 65536

commit v5 on v4

--- a/solution.py
+++ b/solution.py
@@ -280,7 +280,7 @@
                 up = face(es[t][0, first - 1, pl.ds(r, 8)] + es[t][0, first, pl.ds(r, 8)])
                 fzs[t][first, pl.ds(r, 8)] = up
                 below.append(up)
-        step = 2 if (end - first) % 2 == 0 else 1
+        step = 4
 
         def some(j, below):
             for u in range(step):
@@ -407,6 +407,7 @@
 
     def sweep(k):
         first, end = 2 + k, EZ - 2 - k
+        unroll = next(n for n in (5, 4, 3, 2) if (end - first) % n == 0)
         keep, push = coeffs[k]
         rows_of = tiles if k + 1 < FINE_SWEEPS else [X0 + 8 * i for i in range(4)]
         lanes = (0, 1) if k + 1 < FINE_SWEEPS else (0,)
@@ -415,8 +416,8 @@
         def step(j, fluxes):
             fluxes = list(fluxes)
             for i, r in enumerate(rows_of):
-                for u in (0, 1):
-                    p = first + 2 * j + u
+                for u in range(unroll):
+                    p = first + unroll * j + u
                     c = at_rows(ss, p, r, k)
                     left, right = y_low(c), y_high(c)
                     for t in lanes:
@@ -439,7 +440,7 @@
                 fluxes.append(
                     fzs[t][first, pl.ds(r, 8)] * (ss[t][k, first, pl.ds(r, 8)] - ss[t][k, first - 1, pl.ds(r, 8)])
                 )
-        lax.fori_loop(0, (end - first) // 2, step, tuple(fluxes))
+        lax.fori_loop(0, (end - first) // unroll, step, tuple(fluxes))
 
     sweep(0)
     sweep(1)
@@ -506,7 +507,7 @@
         r_first = min(8 - halo, KX + 7 - 8 * n_tiles)
         rows_of = [r_first + 8 * i for i in range(n_tiles)]
         keep, push = ccoeffs[k]
-        unroll = 4 if count % 4 == 0 else 2
+        unroll = count // 2
 
         def step(j, fluxes):
             fluxes = list(fluxes)

time: 56.1 us -> 53.6 us (0.955)
  the two profiles are of different devices: /device:TPU:113 before, /device:TPU:89 now
where the time goes in v5:
time: 53.6 us; the launch traced here: 53.5 us
  Pallas kernels  51.5 us (96%)
  local copies, waits for them, and re-layouts  1.33 us (2%)
  between operations  0.64 us (1%)
    pallas_call x1, Pallas kernels, body(): pl.pallas_call(kernel, out_shape=(jax.ShapeDtypeStruct((NZ, 1, BX, BY), j...  51.5 us
    unnamed x2, local copies, waits for them, and re-layouts  1.33 us

profile of v5, /device:TPU:89, one launch (start us, length us, event | category | flops | bytes accessed | tf_op | source)
XLA Modules:
  0.0 53.5 jit_solution(11298985453031203990)
XLA Ops:
  0.6 51.5 %vcycle.1 = (f32[16,1,32,128]{3,2,1,0:T(8,128)S(1)}, f32[8,1,16,64]{3,2,1,0:T(8,128)S(1)}) custom-call(f32[16,1,32,128]{3,2,1,0:T(8,128)} %right_ref.1, s32[16,1,32,128]{3,2,1,0:T(8,128)} %phase_ref.1, f32[16,1,32,128]{3,2,1,0:T(8,128)} %scale_ref.1), custom_call_target="tpu_custom_call" | custom-call | tf_op jit(solution)/shard_map/vcycle/pallas_call | solution.py:568
  52.1 0.7 %copy.7 = f32[16,1,32,128]{3,2,1,0:T(8,128)} copy(f32[16,1,32,128]{3,2,1,0:T(8,128)S(1)} %get-tuple-element.4) | data formatting | bytes 524288
  52.8 0.6 %copy.8 = f32[8,1,16,64]{3,2,1,0:T(8,128)} copy(f32[8,1,16,64]{3,2,1,0:T(8,128)S(1)} %get-tuple-element.5) | data formatting | bytes 65536
